TPU v7x, 128 devices: a whole 4x4x4 slice. The times are simulated.
128 devices in a mesh: row: 8 (over z_lo, y), col: 16 (over x, z_hi, core).
Axes of the slice: x: 4, y: 4, z: 4 (z_hi: 2, z_lo: 2; z = z_hi * 2 + z_lo), core: 2. Of those that a mesh axis runs over, the one named last changes fastest.
Arguments:
- pressure: float32 [512, 256, 512], P('row', 'col'), may hold values from -4.5 to 4.5
- pressure_prior: float32 [512, 256, 512], P('row', 'col'), may hold values from -6 to 6
- lossy_prior: float32 [512, 256, 512], P('row', 'col'), may hold values from -12 to 12
- stiffness: float32 [512, 256, 512], P('row', 'col'), may hold values from 0.01 to 0.05
- compensation: float32 [512, 256, 512], P('row', 'col'), may hold values from 0.05 to 0.2
- snapshot: float32 [512, 256, 512], P('row', 'col'), may hold values from -6 to 6
- image_prior: float32 [512, 256, 512], P('row', 'col'), may hold values from -6 to 6
Outputs:
- pressure_next: float32 [512, 256, 512], P('row', 'col')
- lossy_term: float32 [512, 256, 512], P('row', 'col')
- image_sum: float32 [512, 256, 512], P('row', 'col')
All inputs are finite; a program needn't handle non-finite values.
Results may differ from a plain program's by a relative error of at most 0.00013.
Values sent between devices are 32-bit elements; how exact they have to be, the bound alone decides.
No kernel may reach another device: no remote copies, remote signals or barrier semaphores. Data moves between devices by JAX's collectives and lax.ppermute only.
A program may use at most 128 MiB of HBM per device.

v0:
```python
import functools
import math

import jax
import jax.numpy as jnp
import ml_dtypes
import numpy as np
from jax import lax
from jax.experimental import pallas as pl
from jax.experimental.pallas import tpu as pltpu
from jax.sharding import PartitionSpec as P

stiff_power = 1.03
lossy_power = 0.53
filter_rate = 0.14
MIB = 1 << 20


def split_table(table):
    high = table.astype(ml_dtypes.bfloat16)
    low = (table - high.astype(np.float64)).astype(ml_dtypes.bfloat16)
    return high, low


def cas(left, right, length):
    angle = 2.0 * math.pi / length * (np.outer(left, right) % length)
    return np.cos(angle) + np.sin(angle)


def left_table(table):
    high, low = split_table(table)
    return np.concatenate([high, high, low], axis=1)


def right_table(table):
    high, low = split_table(table)
    return np.concatenate([high, high, low], axis=0)


def pieces(values):
    high = values.astype(jnp.bfloat16)
    low = (values - high.astype(jnp.float32)).astype(jnp.bfloat16)
    return high, low


def times_table(values, table):
    high, low = pieces(values)
    return jnp.dot(jnp.concatenate([high, low, high], axis=1), table, preferred_element_type=jnp.float32)


def table_times(table, values):
    high, low = pieces(values)
    return jnp.dot(table, jnp.concatenate([high, low, high], axis=0), preferred_element_type=jnp.float32)


def table_times_rows(table, values):
    high, low = pieces(values)
    return lax.dot_general(
        table,
        jnp.concatenate([high, low, high], axis=1),
        (((1,), (1,)), ((), ())),
        preferred_element_type=jnp.float32,
    )


def swap_halves(first, second):
    lane = lax.broadcasted_iota(jnp.int32, first.shape, 1)
    left = jnp.where(lane < 64, first, pltpu.roll(second, 64, 1))
    right = jnp.where(lane < 64, pltpu.roll(first, 64, 1), second)
    return left, right


def side(parts):
    return jnp.concatenate(parts, axis=1)


def forward_x_kernel(pressure, even_left, odd_left, sent, field, packed, in_sems, out_sems):
    def load(h, g):
        return pltpu.make_async_copy(
            pressure.at[:, h, :, pl.ds(g * 128, 128)], field.at[h, g], in_sems.at[h, g]
        )

    def store(h, p):
        return pltpu.make_async_copy(packed.at[h, p], sent.at[:, p, h], out_sems.at[h, p])

    for h in range(2):
        for g in range(4):
            load(h, g).start()
    for h in range(2):
        for g in range(4):
            load(h, g).wait()
        views = [field.at[h, g].reshape(512, 128) for g in range(4)]
        outs = [packed.at[h, p].reshape(1024, 128) for p in range(2)]
        for group in range(2):
            columns = [
                jnp.concatenate([v[pl.ds(group * 4 + i, 64, stride=8), :] for i in range(4)], axis=0)
                for v in views
            ]
            near, far = side(columns[:2]), side(columns[2:])
            products = [
                table_times_rows(even_left[...], near + far),
                table_times_rows(odd_left[...], near - far),
            ]
            for p in range(2):
                for pair in range(2):
                    lanes = slice(pair * 128, pair * 128 + 128)
                    both = swap_halves(products[p][:128, lanes], products[p][128:, lanes])
                    for i in range(2):
                        z = group * 4 + pair * 2 + i
                        outs[p][pl.ds(z, 128, stride=8), :] = both[i]
        for p in range(2):
            store(h, p).start()
    for h in range(2):
        for p in range(2):
            store(h, p).wait()


def plane_kernel(
    received,
    multipliers,
    z_left,
    even_right,
    odd_right,
    odd_back,
    sent,
    planes,
    spectrum,
    filters,
    filtered,
    fields,
    in_sems,
    filter_sems,
    out_sems,
):
    def load(r, p):
        return pltpu.make_async_copy(received.at[r, :, p], planes.at[r, p], in_sems.at[r, p])

    def load_filter(f, k):
        return pltpu.make_async_copy(multipliers.at[f, k], filters.at[f, k], filter_sems.at[f, k])

    def store(r, f, p):
        return pltpu.make_async_copy(
            fields.at[r, f, p], sent.at[r, :, f, p], out_sems.at[r, f, p]
        )

    for r in range(8):
        for p in range(2):
            load(r, p).start()
    for k in range(4):
        for f in range(2):
            load_filter(f, k).start()
    for r in range(8):
        for p in range(2):
            load(r, p).wait()
        plane = side([planes[r, p].reshape(256, 128) for p in range(2)])
        spectrum[r] = table_times(z_left[...], plane)
    for p in range(2):
        lanes = slice(p * 128, p * 128 + 128)
        columns = [[], []]
        for r in range(0, 8, 2):
            both = swap_halves(spectrum[r, :, lanes], spectrum[r + 1, :, lanes])
            for i in range(2):
                columns[i].append(both[i])
        backs = [[], []]
        for i in range(2):
            k = p * 2 + i
            near, far = side(columns[i][:2]), side(columns[i][2:])
            even = times_table(near + far, even_right[...])
            odd = times_table(near - far, odd_right[...])
            for f in range(2):
                load_filter(f, k).wait()
                back_even = times_table(even * filters[f, k, :, :256], even_right[...])
                back_odd = times_table(odd * filters[f, k, :, 256:], odd_back[...])
                backs[f].append(side([back_even + back_odd, back_even - back_odd]))
        for f in range(2):
            for r in range(0, 8, 2):
                part = slice(r * 64, r * 64 + 128)
                both = swap_halves(backs[f][0][:, part], backs[f][1][:, part])
                for i in range(2):
                    filtered[f, r + i, :, lanes] = both[i]
    for r in range(8):
        for f in range(2):
            field = table_times(z_left[...], filtered[f, r])
            for p in range(2):
                fields[r, f, p] = field[:, p * 128 : p * 128 + 128].reshape(16, 16, 128)
                store(r, f, p).start()
    for r in range(8):
        for f in range(2):
            for p in range(2):
                store(r, f, p).wait()


def update_kernel(
    received,
    even_right,
    odd_back,
    pressure,
    pressure_prior,
    lossy_prior,
    stiffness,
    compensation,
    snapshot,
    image_prior,
    pressure_next,
    lossy_term,
    image_sum,
    parts,
    terms,
    inputs,
    outputs,
    part_sems,
    in_sems,
    out_sems,
):
    sources = (
        pressure, pressure_prior, lossy_prior, stiffness, compensation, snapshot, image_prior
    )
    targets = (pressure_next, lossy_term, image_sum)

    def load_part(h, f, p):
        return pltpu.make_async_copy(received.at[:, f, p, h], parts.at[h, f, p], part_sems.at[h, f, p])

    def load(h, a):
        return pltpu.make_async_copy(sources[a].at[:, h], inputs.at[h, a], in_sems.at[h, a])

    def store(h, a):
        return pltpu.make_async_copy(outputs.at[h, a], targets[a].at[:, h], out_sems.at[h, a])

    for h in range(2):
        for f in range(2):
            for p in range(2):
                load_part(h, f, p).start()
        for a in range(7):
            load(h, a).start()
    for h in range(2):
        for f in range(2):
            for p in range(2):
                load_part(h, f, p).wait()
            views = [parts.at[h, f, p].reshape(1024, 128) for p in range(2)]
            for group in range(2):
                rows = [[], []]
                for i in range(4):
                    for p in range(2):
                        block = views[p][pl.ds(group * 4 + i, 128, stride=8), :].T
                        rows[p].append(side([block[:64], block[64:]]))
                even = times_table(jnp.concatenate(rows[0], axis=0), even_right[...])
                odd = times_table(jnp.concatenate(rows[1], axis=0), odd_back[...])
                both = side([even + odd, even - odd])
                for g in range(4):
                    for i in range(4):
                        terms[f, g, pl.ds(group * 4 + i, 64, stride=8), :] = both[
                            i * 64 : i * 64 + 64, g * 128 : g * 128 + 128
                        ]
        for a in range(7):
            load(h, a).wait()

        def step(y, carry):
            mine = pl.ds(pl.multiple_of(y * 64, 64), 64)
            there = pl.ds(y * 8, 8)
            stiff = side([terms[0, g, mine, :] for g in range(4)]).reshape(8, 8, 512)
            lossy = side([terms[1, g, mine, :] for g in range(4)]).reshape(8, 8, 512)
            now, prior, loss, stiffs, comp, snap, image = [inputs[h, a, there] for a in range(7)]
            value = 2.0 * now - prior - stiffs * stiff + comp * (lossy - loss)
            outputs[h, 0, there] = value
            outputs[h, 1, there] = lossy
            outputs[h, 2, there] = image + snap * value
            return carry

        lax.fori_loop(0, 8, step, 0)
        for a in range(3):
            store(h, a).start()
    for h in range(2):
        for a in range(3):
            store(h, a).wait()


def call(kernel, operands, blocks, out_shape, scratch):
    anywhere = pl.BlockSpec(memory_space=pl.ANY)
    table = pl.BlockSpec(memory_space=pltpu.VMEM)
    specs = [table if i in blocks else anywhere for i in range(len(operands))]
    return pl.pallas_call(
        kernel,
        in_specs=specs,
        out_specs=jax.tree.map(lambda _: anywhere, out_shape),
        out_shape=out_shape,
        scratch_shapes=scratch,
        compiler_params=pltpu.CompilerParams(vmem_limit_bytes=56 * MIB),
    )(*operands)


def wave_square(indices, length):
    folded = jnp.minimum(indices, length - indices)
    return (2.0 * math.pi / length * folded.astype(jnp.float32)) ** 2


def body(pressure, pressure_prior, lossy_prior, stiffness, compensation, snapshot, image_prior):
    axes = ("row", "col")
    half = np.arange(256)
    even_table = cas(half, half, 256)
    odd_table = cas(2 * half + 1, half, 512)
    even_left, odd_left = left_table(even_table), left_table(odd_table)
    even_right = right_table(even_table)
    odd_right, odd_back = right_table(odd_table.T), right_table(odd_table)
    z_left = even_left
    arrays = [
        a.reshape(64, 2, 8, 512)
        for a in (pressure, pressure_prior, lossy_prior, stiffness, compensation, snapshot, image_prior)
    ]
    f32 = jnp.float32
    dma = pltpu.SemaphoreType.DMA

    sent = call(
        forward_x_kernel,
        (arrays[0], even_left, odd_left),
        (1, 2),
        jax.ShapeDtypeStruct((128, 2, 2, 8, 128), f32),
        [
            pltpu.VMEM((2, 4, 64, 8, 128), f32),
            pltpu.VMEM((2, 2, 128, 8, 128), f32),
            dma((2, 4)),
            dma((2, 2)),
        ],
    )
    received = lax.all_to_all(sent.reshape(128, 32, 128), axes, split_axis=0, concat_axis=0, tiled=True)

    device = lax.axis_index("row") * 16 + lax.axis_index("col")
    part = jnp.arange(4, dtype=jnp.int32)
    index_x = 2 * (part % 2 * 128 + device) + part // 2
    even_indices = 2 * jnp.arange(256, dtype=jnp.int32)
    index_y = jnp.concatenate([even_indices, even_indices + 1])
    index_z = jnp.arange(256, dtype=jnp.int32)
    squared = (
        wave_square(index_y, 512)[None, None, :]
        + wave_square(index_z, 256)[None, :, None]
        + wave_square(index_x, 512)[:, None, None]
    )
    normalizer = 1.0 / (512 * 256 * 512)
    multipliers = jnp.stack(
        [
            squared**stiff_power * normalizer,
            squared**lossy_power * jnp.exp(-filter_rate * squared) * normalizer,
        ]
    )

    sent = call(
        plane_kernel,
        (received.reshape(8, 16, 2, 16, 128), multipliers, z_left, even_right, odd_right, odd_back),
        (2, 3, 4, 5),
        jax.ShapeDtypeStruct((8, 16, 2, 2, 16, 128), f32),
        [
            pltpu.VMEM((8, 2, 16, 16, 128), f32),
            pltpu.VMEM((8, 256, 256), f32),
            pltpu.VMEM((2, 4, 256, 512), f32),
            pltpu.VMEM((2, 8, 256, 256), f32),
            pltpu.VMEM((8, 2, 2, 16, 16, 128), f32),
            dma((8, 2)),
            dma((2, 4)),
            dma((8, 2, 2)),
        ],
    )
    received = lax.all_to_all(sent.reshape(128, 64, 128), axes, split_axis=0, concat_axis=0, tiled=True)

    outs = call(
        update_kernel,
        (received.reshape(128, 2, 2, 2, 8, 128), even_right, odd_back, *arrays),
        (1, 2),
        [jax.ShapeDtypeStruct((64, 2, 8, 512), f32)] * 3,
        [
            pltpu.VMEM((2, 2, 2, 128, 8, 128), f32),
            pltpu.VMEM((2, 4, 512, 128), f32),
            pltpu.VMEM((2, 7, 64, 8, 512), f32),
            pltpu.VMEM((2, 3, 64, 8, 512), f32),
            dma((2, 2, 2)),
            dma((2, 7)),
            dma((2, 3)),
        ],
    )
    return tuple(o.reshape(64, 16, 512) for o in outs)


def solution(mesh):
    spec = P("row", "col", None)
    return jax.shard_map(
        body, mesh=mesh, in_specs=(spec,) * 7, out_specs=(spec,) * 3, check_vma=False
    )
```

profile of v0, /device:TPU:1, one launch (start us, length us, event | category | flops | bytes accessed | tf_op | source)
XLA Modules:
  0.0 131.0 jit_solution(18263149729724217399)
XLA Ops:
  0.6 5.1 %shard_map.139 = f32[128,2,2,8,128]{4,3,2,1,0:T(8,128)} custom-call(f32[64,2,8,512]{3,2,1,0:T(8,128)} %bitcast.16, bf16[256,768]{1,0:T(8,128)(2,1)} %constant.73.clone.even_left.z_left, bf16[256,768]{1,0:T(8,128)(2,1)} %constant.74.clone.odd_left), custom_call_target="tpu_custom_call" | custom-call | tf_op jit(solution)/shard_map/pallas_call | solution.py:281
  5.8 11.5 %all-to-all-start = ((f32[128,32,128]{2,1,0:T(8,128)}), f32[128,32,128]{2,1,0:T(8,128)S(1)}, u32[]{:S(2)}, u32[]{:S(2)}) async-start(f32[128,32,128]{2,1,0:T(8,128)} %bitcast.18), calls=%async_computation | async-start | bytes 4194304 | tf_op jit(solution)/shard_map/all_to_all | solution.py:324
  17.4 0.1 broadcast_add_fusion
  17.5 2.0 %fusion = (f32[1,4,256,512]{3,2,1,0:T(8,128)S(1)}, f32[1,4,256,512]{3,2,1,0:T(8,128)S(1)}) fusion(f32[4]{0:T(128)S(1)} %fusion.13, f32[256,512]{1,0:T(8,128)S(1)} %broadcast_add_fusion), kind=kLoop, calls=%fused_computation.4 | loop fusion | flops 2621440 | bytes 4718608 | tf_op jit(solution)/shard_map/mul | solution.py:340
  19.5 2.7 %pad_maximum_fusion.multipliers = f32[2,4,256,512]{3,2,1,0:T(8,128)} fusion(f32[1,4,256,512]{3,2,1,0:T(8,128)S(1)} %get-tuple-element.10, f32[1,4,256,512]{3,2,1,0:T(8,128)S(1)} %get-tuple-element.9), kind=kLoop, calls=%fused_computation | loop fusion | flops 1048576 | bytes 8388608 | tf_op jit(solution)/shard_map/stack | solution.py:338
  22.2 25.2 %all-to-all-done = f32[128,32,128]{2,1,0:T(8,128)S(1)} async-done(((f32[128,32,128]{2,1,0:T(8,128)}), f32[128,32,128]{2,1,0:T(8,128)S(1)}, u32[]{:S(2)}, u32[]{:S(2)}) %all-to-all-start) | async-done | bytes 2097184 | tf_op jit(solution)/shard_map/all_to_all | solution.py:324
  47.4 0.0 copy-start
  47.4 1.3 %copy-done = f32[128,32,128]{2,1,0:T(8,128)} copy-done((f32[128,32,128]{2,1,0:T(8,128)}, f32[128,32,128]{2,1,0:T(8,128)S(1)}, u32[]{:S(2)}) %copy-start) | copy-done | bytes 2097176
  48.7 12.9 %shard_map.140 = f32[8,16,2,2,16,128]{5,4,3,2,1,0:T(8,128)} custom-call(f32[8,16,2,16,128]{4,3,2,1,0:T(8,128)} %bitcast.19, f32[2,4,256,512]{3,2,1,0:T(8,128)} %pad_maximum_fusion.multipliers, bf16[256,768]{1,0:T(8,128)(2,1)} %constant.73.clone.even_left.z_left, bf16[768,256]{1,0:T(8,128)(2,1)} %constant.75.clone.even_right, ...), custom_call_target="tpu_custom_call" | custom-call | tf_op jit(solution)/shard_map/pallas_call | solution.py:281
  61.6 58.2 %all_to_all.10 = f32[128,64,128]{2,1,0:T(8,128)} all-to-all(f32[128,64,128]{2,1,0:T(8,128)} %bitcast.15), channel_id=1, replica_groups=mesh['row'=8,'col'=16] {'row','col'}, dimensions={0} | all-to-all | bytes 8388608 | tf_op jit(solution)/shard_map/all_to_all | solution.py:361
  119.8 11.0 %shard_map.141 = (f32[64,2,8,512]{3,2,1,0:T(8,128)}, f32[64,2,8,512]{3,2,1,0:T(8,128)}, f32[64,2,8,512]{3,2,1,0:T(8,128)}) custom-call(f32[128,2,2,2,8,128]{5,4,3,2,1,0:T(8,128)} %bitcast.14, bf16[768,256]{1,0:T(8,128)(2,1)} %constant.75.clone.even_right, bf16[768,256]{1,0:T(8,128)(2,1)} %constant.77.clone.odd_back, f32[64,2,8,512]{3,2,1,0:T(8,128)} %bitcast.17, ...), custom_call_target="tpu_custom_call" | custom-call | tf_op jit(solution)/shard_map/pallas_call | solution.py:281
  (4 shorter events, 0.0 us)
Async XLA Ops:
  5.8 41.6 %all-to-all-start = ((f32[128,32,128]{2,1,0:T(8,128)}), f32[128,32,128]{2,1,0:T(8,128)S(1)}, u32[]{:S(2)}, u32[]{:S(2)}) async-start(f32[128,32,128]{2,1,0:T(8,128)} %bitcast.18), calls=%async_computation | async-start | bytes 4194304 | tf_op jit(solution)/shard_map/all_to_all | solution.py:324
  47.4 1.3 %copy-start = (f32[128,32,128]{2,1,0:T(8,128)}, f32[128,32,128]{2,1,0:T(8,128)S(1)}, u32[]{:S(2)}) copy-start(f32[128,32,128]{2,1,0:T(8,128)S(1)} %all-to-all-done) | copy-start | bytes 6291460
where the time goes:
time: 132 us; the launch traced here: 131 us
  blocking collectives  58.2 us (44%)
  Pallas kernels  29 us (22%)
  waiting for transfers between devices  25.2 us (19%)
  starting transfers between devices  11.5 us (9%)
  other arithmetic  4.86 us (4%)
  local copies, waits for them, and re-layouts  1.32 us (1%)
    all_to_all x1, blocking collectives, body(): lax.all_to_all(sent.reshape(128, 64, 128), axes, split_axis=0, concat_axi...  58.2 us
    pallas_call x3, Pallas kernels, call(): pl.pallas_call(kernel, in_specs=specs, out_specs=jax.tree.map(lambda _: a...  29 us
    all_to_all x1, waiting for transfers between devices, body(): lax.all_to_all(sent.reshape(128, 32, 128), axes, split_axis=0, concat_axi...  25.2 us
    all_to_all x1, starting transfers between devices, body(): lax.all_to_all(sent.reshape(128, 32, 128), axes, split_axis=0, concat_axi...  11.5 us
    another operation x1, other arithmetic, body(): jnp.stack([squared ** stiff_power * normalizer, squared ** lossy_power *...  2.73 us
  transfers between devices with their start and end apart: 1, of which 1 were waited for; matrix products, arithmetic and copies ran while one was open for 4% of the time, Pallas kernels for 0%

commit v1 on v0

v1 whole, which is shorter than its diff:
```python
import functools
import math

import jax
import jax.numpy as jnp
import ml_dtypes
import numpy as np
from jax import lax
from jax.experimental import pallas as pl
from jax.experimental.pallas import tpu as pltpu
from jax.sharding import PartitionSpec as P

stiff_power = 1.03
lossy_power = 0.53
filter_rate = 0.14
MIB = 1 << 20


def split_table(table):
    high = table.astype(ml_dtypes.bfloat16)
    low = (table - high.astype(np.float64)).astype(ml_dtypes.bfloat16)
    return high, low


def cas(left, right, length):
    angle = 2.0 * math.pi / length * (np.outer(left, right) % length)
    return np.cos(angle) + np.sin(angle)


def pieces(values):
    high = values.astype(jnp.bfloat16)
    low = (values - high.astype(jnp.float32)).astype(jnp.bfloat16)
    return high, low


EVEN, ODD = 0, 2


def cat3(high, low, axis):
    return jnp.concatenate([high, low, high], axis=axis)


def product(left, right, right_dim):
    return lax.dot_general(
        left, right, (((1,), (right_dim,)), ((), ())), preferred_element_type=jnp.float32
    )


def times_table(values, tables, which, transposed=False):
    axis = 1 if transposed else 0
    high, low = tables[which], tables[which + 1]
    table = jnp.concatenate([high, high, low], axis=axis)
    return product(cat3(*pieces(values), 1), table, axis)


def table_times(tables, which, values, transposed=False):
    axis = 1 if transposed else 0
    high, low = tables[which], tables[which + 1]
    table = jnp.concatenate([high, high, low], axis=1)
    return product(table, cat3(*pieces(values), axis), axis)


def loop(count, step):
    for i in range(count):
        step(i, 0)


def swap_halves(first, second):
    lane = lax.broadcasted_iota(jnp.int32, first.shape, 1)
    left = jnp.where(lane < 64, first, pltpu.roll(second, 64, 1))
    right = jnp.where(lane < 64, pltpu.roll(first, 64, 1), second)
    return left, right


def side(parts):
    return jnp.concatenate(parts, axis=1)


def forward_x_kernel(pressure, tables, sent, field, packed, table, in_sems, out_sems, table_sem):
    def load(h, g):
        return pltpu.make_async_copy(
            pressure.at[:, h, :, pl.ds(g * 128, 128)], field.at[h, g], in_sems.at[h, g]
        )

    def store(h, p):
        return pltpu.make_async_copy(packed.at[h, p], sent.at[:, p, h], out_sems.at[h, p])

    load_table = pltpu.make_async_copy(tables, table, table_sem)
    for g in range(4):
        load(0, g).start()
    load_table.start()
    for g in range(4):
        load(1, g).start()
    for h in range(2):
        for g in range(4):
            load(h, g).wait()
        if h == 0:
            load_table.wait()
        views = [field.at[h, g].reshape(512, 128) for g in range(4)]
        for p in range(2):
            target = packed.at[h, p].reshape(1024, 128)
            for group in range(2):
                near, far = [
                    side(
                        [
                            jnp.concatenate(
                                [v[pl.ds(group * 4 + i, 64, stride=8), :] for i in range(4)], axis=0
                            )
                            for v in views[half * 2 : half * 2 + 2]
                        ]
                    )
                    for half in range(2)
                ]
                if p == 0:
                    result = times_table(near + far, table, EVEN)
                else:
                    result = times_table(near - far, table, ODD, True)
                for i in range(4):
                    rows = result[i * 64 : i * 64 + 64]
                    block = jnp.concatenate([rows[:, :128], rows[:, 128:]], axis=0)
                    target[pl.ds(group * 4 + i, 128, stride=8), :] = block.T
            store(h, p).start()
    for h in range(2):
        for p in range(2):
            store(h, p).wait()


def plane_kernel(
    received,
    stiff_filter,
    lossy_filter,
    tables,
    sent,
    spectrum,
    whole,
    filtered,
    filters,
    filter_sems,
):
    def load(f, k):
        source = lossy_filter if f else stiff_filter
        return pltpu.make_async_copy(source.at[k], filters.at[f, k], filter_sems.at[f, k])

    for p in range(2):
        for f in range(2):
            for k in (p * 2, p * 2 + 1):
                load(f, k).start()

    def forward_z(r, carry):
        plane = side([received[r, :, p].reshape(256, 128) for p in range(2)])
        result = table_times(tables, EVEN, plane)
        for p in range(2):
            spectrum[p, r] = result[:, p * 128 : p * 128 + 128]
        return carry

    loop(8, forward_z)

    for p in range(2):
        columns = [[], []]
        for r in range(0, 8, 2):
            both = swap_halves(spectrum[p, r], spectrum[p, r + 1])
            for i in range(2):
                columns[i].append(both[i])
        for i in range(2):
            k = p * 2 + i
            near, far = side(columns[i][:2]), side(columns[i][2:])
            whole[k, :, :256] = times_table(near + far, tables, EVEN)
            whole[k, :, 256:] = times_table(near - far, tables, ODD, True)
    for p in range(2):
        for f in range(2):
            backs = []
            for k in (p * 2, p * 2 + 1):
                load(f, k).wait()
                back_even = times_table(whole[k, :, :256] * filters[f, k, :, :256], tables, EVEN)
                back_odd = times_table(whole[k, :, 256:] * filters[f, k, :, 256:], tables, ODD)
                backs.append(side([back_even + back_odd, back_even - back_odd]))
            for r in range(0, 8, 2):
                part = slice(r * 64, r * 64 + 128)
                both = swap_halves(backs[0][:, part], backs[1][:, part])
                for i in range(2):
                    filtered[f, r + i, p] = both[i]

    def back_z(r, carry):
        for f in range(2):
            field = table_times(tables, EVEN, side([filtered[f, r, p] for p in range(2)]))
            for p in range(2):
                sent[r, :, f, p] = field[:, p * 128 : p * 128 + 128].reshape(16, 16, 128)
        return carry

    loop(8, back_z)


def update_kernel(
    received,
    tables,
    pressure,
    pressure_prior,
    lossy_prior,
    stiffness,
    compensation,
    snapshot,
    image_prior,
    pressure_next,
    lossy_term,
    image_sum,
    terms,
    outputs,
    out_sems,
):
    sources = (
        pressure, pressure_prior, lossy_prior, stiffness, compensation, snapshot, image_prior
    )
    targets = (pressure_next, lossy_term, image_sum)

    def store(h, a, part):
        mine = pl.ds(part * 16, 16)
        return pltpu.make_async_copy(
            outputs.at[h, a, mine], targets[a].at[mine, h], out_sems.at[h, a, part]
        )

    for h in range(2):
        for f in (1, 0):
            for group in range(2):
                rows = [[], []]
                for i in range(4):
                    for p in range(2):
                        place = f * 32 + p * 16 + h * 8 + group * 4 + i
                        block = received[pl.ds(place, 128, stride=64), :].T
                        rows[p].append(side([block[:64], block[64:]]))
                even = times_table(jnp.concatenate(rows[0], axis=0), tables, EVEN)
                odd = times_table(jnp.concatenate(rows[1], axis=0), tables, ODD)
                both = side([even + odd, even - odd])
                for g in range(4):
                    for i in range(4):
                        terms[f, g, pl.ds(group * 4 + i, 64, stride=8), :] = both[
                            i * 64 : i * 64 + 64, g * 128 : g * 128 + 128
                        ]
            if f:
                for part in range(4):
                    for y in range(part * 2, part * 2 + 2):
                        mine = pl.ds(y * 64, 64)
                        lossy = side([terms[1, g, mine, :] for g in range(4)])
                        outputs[h, 1, pl.ds(y * 8, 8)] = lossy.reshape(8, 8, 512)
                    store(h, 1, part).start()
        for part in range(4):
            for y in range(part * 2, part * 2 + 2):
                mine = pl.ds(y * 64, 64)
                there = pl.ds(y * 8, 8)
                stiff = side([terms[0, g, mine, :] for g in range(4)]).reshape(8, 8, 512)
                lossy = outputs[h, 1, there]
                now, prior, loss, stiffs, comp, snap, image = [s[there, h] for s in sources]
                value = 2.0 * now - prior - stiffs * stiff + comp * (lossy - loss)
                outputs[h, 0, there] = value
                outputs[h, 2, there] = image + snap * value
            store(h, 0, part).start()
            store(h, 2, part).start()
    for h in range(2):
        for a in range(3):
            for part in range(4):
                store(h, a, part).wait()


def held(array):
    return pltpu.with_memory_space_constraint(array, pltpu.VMEM)


def outer(array):
    return pltpu.with_memory_space_constraint(array, pltpu.HBM)


def call(kernel, operands, outside, out_shape, scratch, limit):
    anywhere = pl.BlockSpec(memory_space=pl.ANY)
    vmem = pl.BlockSpec(memory_space=pltpu.VMEM)
    return pl.pallas_call(
        kernel,
        in_specs=[anywhere if i in outside else vmem for i in range(len(operands))],
        out_specs=jax.tree.map(
            lambda s: anywhere if isinstance(s, jax.ShapeDtypeStruct) else vmem, out_shape
        ),
        out_shape=out_shape,
        scratch_shapes=scratch,
        compiler_params=pltpu.CompilerParams(vmem_limit_bytes=limit * MIB),
    )(*operands)


def wave_square(indices, length):
    folded = jnp.minimum(indices, length - indices)
    return (2.0 * math.pi / length * folded.astype(jnp.float32)) ** 2


def body(pressure, pressure_prior, lossy_prior, stiffness, compensation, snapshot, image_prior):
    axes = ("row", "col")
    half = np.arange(256)
    even_table = cas(half, half, 256)
    odd_table = cas(2 * half + 1, half, 512)
    tables = np.stack([*split_table(even_table), *split_table(odd_table)])
    arrays = [
        a.reshape(64, 2, 8, 512)
        for a in (pressure, pressure_prior, lossy_prior, stiffness, compensation, snapshot, image_prior)
    ]
    f32 = jnp.float32
    dma = pltpu.SemaphoreType.DMA

    sent = call(
        forward_x_kernel,
        (outer(arrays[0]), outer(tables)),
        (0, 1),
        jax.ShapeDtypeStruct((128, 2, 2, 8, 128), f32),
        [
            pltpu.VMEM((2, 4, 64, 8, 128), f32),
            pltpu.VMEM((2, 2, 128, 8, 128), f32),
            pltpu.VMEM((4, 256, 256), jnp.bfloat16),
            dma((2, 4)),
            dma((2, 2)),
            dma,
        ],
        12,
    )
    received = lax.all_to_all(sent.reshape(128, 32, 128), axes, split_axis=0, concat_axis=0, tiled=True)

    device = lax.axis_index("row") * 16 + lax.axis_index("col")
    part = jnp.arange(4, dtype=jnp.int32)
    index_x = 2 * (part % 2 * 128 + device) + part // 2
    even_indices = 2 * jnp.arange(256, dtype=jnp.int32)
    index_y = jnp.concatenate([even_indices, even_indices + 1])
    index_z = jnp.arange(256, dtype=jnp.int32)
    squared = (
        wave_square(index_y, 512)[None, None, :]
        + wave_square(index_z, 256)[None, :, None]
        + wave_square(index_x, 512)[:, None, None]
    )
    normalizer = 1.0 / (512 * 256 * 512)
    stiff_filter = squared**stiff_power * normalizer
    lossy_filter = squared**lossy_power * jnp.exp(-filter_rate * squared) * normalizer

    sent = call(
        plane_kernel,
        (
            held(received.reshape(8, 16, 2, 16, 128)),
            outer(stiff_filter),
            outer(lossy_filter),
            held(tables),
        ),
        (1, 2),
        pltpu.VMEM((8, 16, 2, 2, 16, 128), f32),
        [
            pltpu.VMEM((2, 8, 256, 128), f32),
            pltpu.VMEM((4, 256, 512), f32),
            pltpu.VMEM((2, 8, 2, 256, 128), f32),
            pltpu.VMEM((2, 4, 256, 512), f32),
            dma((2, 4)),
        ],
        16,
    )
    received = lax.all_to_all(sent.reshape(128, 64, 128), axes, split_axis=0, concat_axis=0, tiled=True)

    outs = call(
        update_kernel,
        (held(received.reshape(8192, 128)), held(tables), *map(held, arrays)),
        (),
        [jax.ShapeDtypeStruct((64, 2, 8, 512), f32)] * 3,
        [
            pltpu.VMEM((2, 4, 512, 128), f32),
            pltpu.VMEM((2, 3, 64, 8, 512), f32),
            dma((2, 3, 4)),
        ],
        16,
    )
    return tuple(o.reshape(64, 16, 512) for o in outs)


def solution(mesh):
    spec = P("row", "col", None)
    return jax.shard_map(
        body, mesh=mesh, in_specs=(spec,) * 7, out_specs=(spec,) * 3, check_vma=False
    )
```

time: 132 us -> 121 us (0.917)
  Pallas kernels: 29 us -> 18.7 us
    pallas_call x3, Pallas kernels: 29 us -> 18.7 us  [call(): pl.pallas_call(kernel, in_specs=[anywhere if i in outside else vmem for i...]
    another operation x1 -> x0, other arithmetic: 2.73 us -> none  [body(): jnp.stack([squared ** stiff_power * normalizer, squared ** lossy_power *...]
    mul x1, other arithmetic: 1.99 us -> 3.98 us  [body(): squared ** lossy_power * jnp.exp(-filter_rate * squared) * normalizer]
  transfers between devices with their start and end apart: 1 -> 1, of which waited for: 1 -> 1; matrix products, arithmetic and copies ran while one was open for 4% -> 3% of each run, Pallas kernels for 0% -> 0%
where the time goes in v1:
time: 121 us; the launch traced here: 119 us
  blocking collectives  58 us (48%)
  waiting for transfers between devices  25.9 us (21%)
  Pallas kernels  18.7 us (15%)
  starting transfers between devices  11.5 us (10%)
  other arithmetic  4.12 us (3%)
    all_to_all x1, blocking collectives, body(): lax.all_to_all(sent.reshape(128, 64, 128), axes, split_axis=0, concat_axi...  58 us
    all_to_all x1, waiting for transfers between devices, body(): lax.all_to_all(sent.reshape(128, 32, 128), axes, split_axis=0, concat_axi...  25.9 us
    pallas_call x3, Pallas kernels, call(): pl.pallas_call(kernel, in_specs=[anywhere if i in outside else vmem for i...  18.7 us
    all_to_all x1, starting transfers between devices, body(): lax.all_to_all(sent.reshape(128, 32, 128), axes, split_axis=0, concat_axi...  11.5 us
    mul x1, other arithmetic, body(): squared ** lossy_power * jnp.exp(-filter_rate * squared) * normalizer  3.98 us
  transfers between devices with their start and end apart: 1, of which 1 were waited for; matrix products, arithmetic and copies ran while one was open for 3% of the time, Pallas kernels for 0%

profile of v1, /device:TPU:1, one launch (start us, length us, event | category | flops | bytes accessed | tf_op | source)
XLA Modules:
  0.0 119.2 jit_solution(5901776859799881254)
XLA Ops:
  0.6 4.4 %shard_map.103 = f32[128,2,2,8,128]{4,3,2,1,0:T(8,128)} custom-call(f32[64,2,8,512]{3,2,1,0:T(8,128)} %bitcast.16, bf16[4,256,256]{2,1,0:T(8,128)(2,1)} %constant.65.clone.tables), custom_call_target="tpu_custom_call" | custom-call | tf_op jit(solution)/shard_map/pallas_call | solution.py:274
  5.0 11.5 %all-to-all-start = ((f32[128,32,128]{2,1,0:T(8,128)}), f32[128,32,128]{2,1,0:T(8,128)S(1)}, u32[]{:S(2)}, u32[]{:S(2)}) async-start(f32[128,32,128]{2,1,0:T(8,128)} %bitcast.1), calls=%async_computation | async-start | bytes 4194304 | tf_op jit(solution)/shard_map/all_to_all | solution.py:319
  16.6 0.1 broadcast_add_fusion
  16.7 0.0 copy-start.1
  16.7 4.0 %fusion.2 = (f32[4,256,512]{2,1,0:T(8,128)}, f32[4,256,512]{2,1,0:T(8,128)}) fusion(f32[4]{0:T(128)S(1)} %fusion.13, f32[256,512]{1,0:T(8,128)S(1)} %broadcast_add_fusion), kind=kLoop, calls=%fused_computation.5 | loop fusion | flops 2621440 | bytes 4718608 | tf_op jit(solution)/shard_map/mul | solution.py:334
  20.7 25.9 %all-to-all-done = f32[128,32,128]{2,1,0:T(8,128)S(1)} async-done(((f32[128,32,128]{2,1,0:T(8,128)}), f32[128,32,128]{2,1,0:T(8,128)S(1)}, u32[]{:S(2)}, u32[]{:S(2)}) %all-to-all-start) | async-done | bytes 2097184 | tf_op jit(solution)/shard_map/all_to_all | solution.py:319
  46.6 0.0 copy-done.1
  46.6 0.0 copy-start.5
  46.6 0.0 copy-start.6
  46.6 0.0 copy-start.7
  46.6 7.6 %shard_map.104 = f32[8,16,2,2,16,128]{5,4,3,2,1,0:T(8,128)S(1)} custom-call(f32[8,16,2,16,128]{4,3,2,1,0:T(8,128)S(1)} %bitcast.18, f32[4,256,512]{2,1,0:T(8,128)} %get-tuple-element.10.stiff_filter, f32[4,256,512]{2,1,0:T(8,128)} %get-tuple-element.9.lossy_filter, bf16[4,256,256]{2,1,0:T(8,128)(2,1)S(1)} %copy-done.1), custom_call_target="tpu_custom_call" | custom-call | tf_op jit(solution)/shard_map/pallas_call | solution.py:274
  54.2 0.0 copy-start
  54.2 0.0 copy-start.2
  54.2 0.0 copy-start.3
  54.2 0.0 copy-start.4
  54.2 58.0 %all_to_all.10 = f32[128,64,128]{2,1,0:T(8,128)S(1)} all-to-all(f32[128,64,128]{2,1,0:T(8,128)S(1)} %bitcast.15), channel_id=1, replica_groups=mesh['row'=8,'col'=16] {'row','col'}, dimensions={0} | all-to-all | bytes 8388608 | tf_op jit(solution)/shard_map/all_to_all | solution.py:355
  112.2 0.0 copy-done.5
  112.2 0.0 copy-done.6
  112.2 0.0 copy-done.7
  112.2 0.0 copy-done
  112.2 0.0 copy-done.2
  112.2 0.0 copy-done.3
  112.2 0.0 copy-done.4
  112.2 6.7 %shard_map.105 = (f32[64,2,8,512]{3,2,1,0:T(8,128)}, f32[64,2,8,512]{3,2,1,0:T(8,128)}, f32[64,2,8,512]{3,2,1,0:T(8,128)}) custom-call(f32[8192,128]{1,0:T(8,128)S(1)} %bitcast.14, bf16[4,256,256]{2,1,0:T(8,128)(2,1)S(1)} %copy-done.1, f32[64,2,8,512]{3,2,1,0:T(8,128)S(1)} %bitcast.17, f32[64,2,8,512]{3,2,1,0:T(8,128)S(1)} %bitcast.19, ...), custom_call_target="tpu_custom_call" | custom-call | tf_op jit(solution)/shard_map/pallas_call | solution.py:274
  (4 shorter events, 0.0 us)
Async XLA Ops:
  5.0 41.6 %all-to-all-start = ((f32[128,32,128]{2,1,0:T(8,128)}), f32[128,32,128]{2,1,0:T(8,128)S(1)}, u32[]{:S(2)}, u32[]{:S(2)}) async-start(f32[128,32,128]{2,1,0:T(8,128)} %bitcast.1), calls=%async_computation | async-start | bytes 4194304 | tf_op jit(solution)/shard_map/all_to_all | solution.py:319
  16.7 29.9 %copy-start.1 = (bf16[4,256,256]{2,1,0:T(8,128)(2,1)S(1)}, bf16[4,256,256]{2,1,0:T(8,128)(2,1)}, u32[]{:S(2)}) copy-start(bf16[4,256,256]{2,1,0:T(8,128)(2,1)} %constant.65.clone.tables) | copy-start | bytes 1572868
  46.6 65.6 %copy-start.5 = (f32[64,16,512]{2,1,0:T(8,128)S(1)}, f32[64,16,512]{2,1,0:T(8,128)}, u32[]{:S(2)}) copy-start(f32[64,16,512]{2,1,0:T(8,128)} %param.12) | copy-start | bytes 6291460
  46.6 65.6 %copy-start.6 = (f32[64,16,512]{2,1,0:T(8,128)S(1)}, f32[64,16,512]{2,1,0:T(8,128)}, u32[]{:S(2)}) copy-start(f32[64,16,512]{2,1,0:T(8,128)} %param.13) | copy-start | bytes 6291460
  46.6 65.6 %copy-start.7 = (f32[64,16,512]{2,1,0:T(8,128)S(1)}, f32[64,16,512]{2,1,0:T(8,128)}, u32[]{:S(2)}) copy-start(f32[64,16,512]{2,1,0:T(8,128)} %param.14) | copy-start | bytes 6291460
  54.2 58.0 %copy-start = (f32[64,16,512]{2,1,0:T(8,128)S(1)}, f32[64,16,512]{2,1,0:T(8,128)}, u32[]{:S(2)}) copy-start(f32[64,16,512]{2,1,0:T(8,128)} %param.8) | copy-start | bytes 6291460
  54.2 58.0 %copy-start.2 = (f32[64,16,512]{2,1,0:T(8,128)S(1)}, f32[64,16,512]{2,1,0:T(8,128)}, u32[]{:S(2)}) copy-start(f32[64,16,512]{2,1,0:T(8,128)} %param.9) | copy-start | bytes 6291460
  54.2 58.0 %copy-start.3 = (f32[64,16,512]{2,1,0:T(8,128)S(1)}, f32[64,16,512]{2,1,0:T(8,128)}, u32[]{:S(2)}) copy-start(f32[64,16,512]{2,1,0:T(8,128)} %param.10) | copy-start | bytes 6291460
  54.2 58.0 %copy-start.4 = (f32[64,16,512]{2,1,0:T(8,128)S(1)}, f32[64,16,512]{2,1,0:T(8,128)}, u32[]{:S(2)}) copy-start(f32[64,16,512]{2,1,0:T(8,128)} %param.11) | copy-start | bytes 6291460

commit v2 on v1

v2 whole, which is shorter than its diff:
```python
import functools
import math

import jax
import jax.numpy as jnp
import ml_dtypes
import numpy as np
from jax import lax
from jax.experimental import pallas as pl
from jax.experimental.pallas import tpu as pltpu
from jax.sharding import PartitionSpec as P

stiff_power = 1.03
lossy_power = 0.53
filter_rate = 0.14
MIB = 1 << 20


def split_table(table):
    high = table.astype(ml_dtypes.bfloat16)
    low = (table - high.astype(np.float64)).astype(ml_dtypes.bfloat16)
    return high, low


def cas(left, right, length):
    angle = 2.0 * math.pi / length * (np.outer(left, right) % length)
    return np.cos(angle) + np.sin(angle)


def pieces(values):
    high = values.astype(jnp.bfloat16)
    low = (values - high.astype(jnp.float32)).astype(jnp.bfloat16)
    return high, low


EVEN, ODD, EVEN_BACK = 0, 2, 4


def cat3(high, low, axis):
    return jnp.concatenate([high, low, high], axis=axis)


def product(left, right, right_dim):
    return lax.dot_general(
        left, right, (((1,), (right_dim,)), ((), ())), preferred_element_type=jnp.float32
    )


def times_table(values, tables, which, transposed=False):
    axis = 1 if transposed else 0
    high, low = tables[which], tables[which + 1]
    table = jnp.concatenate([high, high, low], axis=axis)
    return product(cat3(*pieces(values), 1), table, axis)


def table_times(tables, which, values, transposed=False):
    axis = 1 if transposed else 0
    high, low = tables[which], tables[which + 1]
    table = jnp.concatenate([high, high, low], axis=1)
    return product(table, cat3(*pieces(values), axis), axis)


def loop(count, step):
    for i in range(count):
        step(i, 0)


def swap_halves(first, second):
    lane = lax.broadcasted_iota(jnp.int32, first.shape, 1)
    left = jnp.where(lane < 64, first, pltpu.roll(second, 64, 1))
    right = jnp.where(lane < 64, pltpu.roll(first, 64, 1), second)
    return left, right


def side(parts):
    return jnp.concatenate(parts, axis=1)


def write_filters(device, filters):
    normalizer = 1.0 / (512 * 256 * 512)
    lane = lax.broadcasted_iota(jnp.int32, (8, 128), 1)
    row = lax.broadcasted_iota(jnp.int32, (8, 128), 0)
    even_y = 2 * lane
    waves_y = [even_y, jnp.where(lane == 0, 256, even_y), even_y + 1]
    even_x = 2 * device
    waves_x = [even_x, jnp.where(device == 0, 256, even_x), even_x + 1]

    def square(wave, length):
        return (2.0 * math.pi / length * wave.astype(jnp.float32)) ** 2

    squares_y = [square(wave, 512) for wave in waves_y]
    squares_x = [square(wave, 512) for wave in waves_x]
    for tile in range(17):
        wave_z = row + tile * 8 if tile < 16 else jnp.where(row == 0, 128, row)
        square_z = square(wave_z, 256)
        for j in range(3):
            square_yz = squares_y[j] + square_z
            for q in range(3):
                squared = square_yz + squares_x[q]
                logarithm = jnp.log(squared)
                place = (q, slice(tile * 8, tile * 8 + 8), slice(j * 128, j * 128 + 128))
                filters[(0, *place)] = jnp.exp(stiff_power * logarithm) * normalizer
                filters[(1, *place)] = (
                    jnp.exp(lossy_power * logarithm - filter_rate * squared) * normalizer
                )


def forward_x_kernel(device, pressure, tables, sent, filters, field, table, in_sems, table_sem):
    def load(h, g):
        return pltpu.make_async_copy(
            pressure.at[:, h, :, pl.ds(g * 128, 128)], field.at[h, g], in_sems.at[h, g]
        )

    load_table = pltpu.make_async_copy(tables.at[pl.ds(0, 4)], table, table_sem)
    for g in range(4):
        load(0, g).start()
    load_table.start()
    for g in range(4):
        load(1, g).start()
    write_filters(device[0], filters)
    load_table.wait()
    for h in range(2):
        for g in range(4):
            load(h, g).wait()
        views = [field.at[h, g].reshape(512, 128) for g in range(4)]
        for group in range(2):
            near, far = [
                side(
                    [
                        jnp.concatenate(
                            [v[pl.ds(group * 4 + i, 64, stride=8), :] for i in range(4)], axis=0
                        )
                        for v in views[half * 2 : half * 2 + 2]
                    ]
                )
                for half in range(2)
            ]
            results = [
                times_table(near + far, table, EVEN),
                times_table(near - far, table, ODD, True),
            ]
            for p in range(2):
                for i in range(4):
                    rows = results[p][i * 64 : i * 64 + 64]
                    block = jnp.concatenate([rows[:, :128], rows[:, 128:]], axis=0)
                    place = p * 16 + h * 8 + group * 4 + i
                    sent[pl.ds(place, 128, stride=32), :] = block.T


def plane_kernel(received, filters, tables, sent, spectrum, whole, filtered):
    chunks = [(high, x, core) for x in range(4) for high in range(2) for core in range(2)]
    for r in range(8):
        low, y = divmod(r, 4)
        plane = jnp.concatenate(
            [
                side([received[high, low, y, x, core, p] for p in range(2)])
                for high, x, core in chunks
            ],
            axis=0,
        )
        result = table_times(tables, EVEN_BACK, plane)
        for p in range(2):
            spectrum[p, r] = result[:, p * 128 : p * 128 + 128]
    for p in range(2):
        columns = [[], []]
        for r in range(0, 8, 2):
            both = swap_halves(spectrum[p, r], spectrum[p, r + 1])
            for i in range(2):
                columns[i].append(both[i])
        for i in range(2):
            k = p * 2 + i
            near, far = side(columns[i][:2]), side(columns[i][2:])
            whole[k, :, :256] = times_table(near + far, tables, EVEN)
            whole[k, :, 256:] = times_table(near - far, tables, ODD, True)
    for p in range(2):
        for f in range(2):
            backs = []
            for k in (p * 2, p * 2 + 1):
                q = min(k, 2)
                filter_rows = jnp.concatenate(
                    [filters[f, q, 0:128], filters[f, q, 128:136], filters[f, q, 8:128]], axis=0
                )
                filter_odd = side([filter_rows[:, 256:], filter_rows[:, 256:]])
                back_even = times_table(whole[k, :, :256] * filter_rows[:, :256], tables, EVEN_BACK)
                back_odd = times_table(whole[k, :, 256:] * filter_odd, tables, ODD)
                backs.append(side([back_even + back_odd, back_even - back_odd]))
            for r in range(0, 8, 2):
                part = slice(r * 64, r * 64 + 128)
                both = swap_halves(backs[0][:, part], backs[1][:, part])
                for i in range(2):
                    filtered[f, r + i, p] = both[i]
    for r in range(8):
        low, y = divmod(r, 4)
        for f in range(2):
            field = table_times(tables, EVEN, side([filtered[f, r, p] for p in range(2)]))
            for c, (high, x, core) in enumerate(chunks):
                for p in range(2):
                    sent[high, low, y, x, core, f, p] = field[
                        c * 16 : c * 16 + 16, p * 128 : p * 128 + 128
                    ]


def update_kernel(
    received,
    tables,
    pressure,
    pressure_prior,
    lossy_prior,
    stiffness,
    compensation,
    snapshot,
    image_prior,
    pressure_next,
    lossy_term,
    image_sum,
    terms,
    outputs,
    out_sems,
):
    sources = (
        pressure, pressure_prior, lossy_prior, stiffness, compensation, snapshot, image_prior
    )
    targets = (pressure_next, lossy_term, image_sum)

    def store(h, a, part):
        mine = pl.ds(part * 16, 16)
        return pltpu.make_async_copy(
            outputs.at[h, a, mine], targets[a].at[mine, h], out_sems.at[h, a, part]
        )

    for h in range(2):
        for f in (1, 0):
            for group in range(2):
                rows = [[], []]
                for i in range(4):
                    for p in range(2):
                        place = f * 32 + p * 16 + h * 8 + group * 4 + i
                        block = received[pl.ds(place, 128, stride=64), :].T
                        rows[p].append(side([block[:64], block[64:]]))
                even = times_table(jnp.concatenate(rows[0], axis=0), tables, EVEN_BACK)
                odd = times_table(jnp.concatenate(rows[1], axis=0), tables, ODD)
                both = side([even + odd, even - odd])
                for g in range(4):
                    for i in range(4):
                        terms[f, g, pl.ds(group * 4 + i, 64, stride=8), :] = both[
                            i * 64 : i * 64 + 64, g * 128 : g * 128 + 128
                        ]
            if f:
                for part in range(4):
                    for y in range(part * 2, part * 2 + 2):
                        mine = pl.ds(y * 64, 64)
                        lossy = side([terms[1, g, mine, :] for g in range(4)])
                        outputs[h, 1, pl.ds(y * 8, 8)] = lossy.reshape(8, 8, 512)
                    store(h, 1, part).start()
        for part in range(4):
            for y in range(part * 2, part * 2 + 2):
                mine = pl.ds(y * 64, 64)
                there = pl.ds(y * 8, 8)
                stiff = side([terms[0, g, mine, :] for g in range(4)]).reshape(8, 8, 512)
                lossy = outputs[h, 1, there]
                now, prior, loss, stiffs, comp, snap, image = [s[there, h] for s in sources]
                value = 2.0 * now - prior - stiffs * stiff + comp * (lossy - loss)
                outputs[h, 0, there] = value
                outputs[h, 2, there] = image + snap * value
            store(h, 0, part).start()
            store(h, 2, part).start()
    for h in range(2):
        for a in range(3):
            for part in range(4):
                store(h, a, part).wait()


def held(array):
    return pltpu.with_memory_space_constraint(array, pltpu.VMEM)


def outer(array):
    return pltpu.with_memory_space_constraint(array, pltpu.HBM)


def call(kernel, operands, spaces, out_shape, scratch, limit):
    return pl.pallas_call(
        kernel,
        in_specs=[pl.BlockSpec(memory_space=space) for space in spaces],
        out_specs=[
            pl.BlockSpec(memory_space=pl.ANY if isinstance(s, jax.ShapeDtypeStruct) else pltpu.VMEM)
            for s in out_shape
        ],
        out_shape=out_shape,
        scratch_shapes=scratch,
        compiler_params=pltpu.CompilerParams(vmem_limit_bytes=limit * MIB),
    )(*operands)


def exchange(array, order):
    return lax.all_to_all(
        array, ("row", "col"), split_axis=0, concat_axis=0, tiled=True, axis_index_groups=[order]
    )


def body(pressure, pressure_prior, lossy_prior, stiffness, compensation, snapshot, image_prior):
    half = np.arange(256)
    even_order = np.concatenate([half[:128], [128], half[:128:-1]])
    odd_order = np.concatenate([half[:128], half[:127:-1]])
    even_table = cas(half, even_order, 256)
    odd_table = cas(2 * odd_order + 1, half, 512)
    tables = np.stack(
        [*split_table(even_table), *split_table(odd_table), *split_table(even_table.T)]
    )
    place = np.arange(128).reshape(2, 4, 4, 2, 2)
    order = [int(i) for i in place.transpose(3, 0, 1, 2, 4).reshape(-1)]
    row, col = lax.axis_index("row"), lax.axis_index("col")
    device = (col // 2 % 2 * 2 + row // 4) * 32 + row % 4 * 8 + col // 4 * 2 + col % 2
    arrays = [
        a.reshape(64, 2, 8, 512)
        for a in (pressure, pressure_prior, lossy_prior, stiffness, compensation, snapshot, image_prior)
    ]
    f32 = jnp.float32
    dma = pltpu.SemaphoreType.DMA
    vmem = pltpu.VMEM

    sent, filters = call(
        forward_x_kernel,
        (device.reshape(1), outer(arrays[0]), outer(tables)),
        (pltpu.SMEM, pl.ANY, pl.ANY),
        [vmem((4096, 128), f32), vmem((2, 3, 136, 384), f32)],
        [
            vmem((2, 4, 64, 8, 128), f32),
            vmem((4, 256, 256), jnp.bfloat16),
            dma((2, 4)),
            dma,
        ],
        12,
    )
    received = exchange(sent.reshape(128, 32, 128), order)

    (sent,) = call(
        plane_kernel,
        (held(received.reshape(2, 2, 4, 4, 2, 2, 16, 128)), held(filters), held(tables)),
        (vmem, vmem, vmem),
        [vmem((2, 2, 4, 4, 2, 2, 2, 16, 128), f32)],
        [
            vmem((2, 8, 256, 128), f32),
            vmem((4, 256, 512), f32),
            vmem((2, 8, 2, 256, 128), f32),
        ],
        16,
    )
    received = exchange(sent.reshape(128, 64, 128), order)

    outs = call(
        update_kernel,
        (held(received.reshape(8192, 128)), held(tables), *map(held, arrays)),
        (vmem,) * 9,
        [jax.ShapeDtypeStruct((64, 2, 8, 512), f32)] * 3,
        [
            vmem((2, 4, 512, 128), f32),
            vmem((2, 3, 64, 8, 512), f32),
            dma((2, 3, 4)),
        ],
        16,
    )
    return tuple(o.reshape(64, 16, 512) for o in outs)


def solution(mesh):
    spec = P("row", "col", None)
    return jax.shard_map(
        body, mesh=mesh, in_specs=(spec,) * 7, out_specs=(spec,) * 3, check_vma=False
    )
```

time: 121 us -> 117 us (0.967); the launches traced: 119 us -> 117 us
  blocking collectives: 58 us -> 99 us
  waiting for transfers between devices: 25.9 us -> 0 us
  starting transfers between devices: 11.5 us -> 0 us
  other arithmetic: 4.12 us -> 0 us
  Pallas kernels: 18.7 us -> 16.8 us
    all_to_all x1 -> x2, blocking collectives: 58 us -> 99 us  [exchange(): lax.all_to_all(array, ('row', 'col'), split_axis=0, concat_axis=0, tiled=...]
    all_to_all x1 -> x0, waiting for transfers between devices: 25.9 us -> none  [body(): lax.all_to_all(sent.reshape(128, 32, 128), axes, split_axis=0, concat_axi...]
    all_to_all x1 -> x0, starting transfers between devices: 11.5 us -> none  [body(): lax.all_to_all(sent.reshape(128, 32, 128), axes, split_axis=0, concat_axi...]
    mul x2 -> x0, other arithmetic: 3.98 us -> none  [the longest x1 3.98 us: body(): squared ** lossy_power * jnp.exp(-filter_rate * squared) * normalizer]
    pallas_call x3, Pallas kernels: 18.7 us -> 16.8 us  [call(): pl.pallas_call(kernel, in_specs=[pl.BlockSpec(memory_space=space) for spa...]
  transfers between devices with their start and end apart: 1 -> 0, of which waited for: 1 -> 0; matrix products, arithmetic and copies ran while one was open for 3% -> 0% of each run, Pallas kernels for 0% -> 0%
where the time goes in v2:
time: 117 us
  blocking collectives  99 us (85%)
  Pallas kernels  16.8 us (14%)
    all_to_all x2, blocking collectives, exchange(): lax.all_to_all(array, ('row', 'col'), split_axis=0, concat_axis=0, tiled=...  99 us
    pallas_call x3, Pallas kernels, call(): pl.pallas_call(kernel, in_specs=[pl.BlockSpec(memory_space=space) for spa...  16.8 us

profile of v2, /device:TPU:1, one launch (start us, length us, event | category | flops | bytes accessed | tf_op | source)
XLA Modules:
  0.0 116.8 jit_solution(8316306710561498762)
XLA Ops:
  0.7 4.3 %shard_map.103 = (f32[4096,128]{1,0:T(8,128)S(1)}, f32[2,3,136,384]{3,2,1,0:T(8,128)S(1)}) custom-call(s32[1]{0:T(128)} %bitcast.device, f32[64,2,8,512]{3,2,1,0:T(8,128)} %bitcast.17, bf16[6,256,256]{2,1,0:T(8,128)(2,1)} %constant.68.clone.tables), custom_call_target="tpu_custom_call" | custom-call | tf_op jit(solution)/shard_map/pallas_call | solution.py:282
  5.0 0.0 copy-start.1
  5.0 41.8 %all_to_all.10 = f32[128,32,128]{2,1,0:T(8,128)S(1)} all-to-all(f32[128,32,128]{2,1,0:T(8,128)S(1)} %bitcast.26), channel_id=1, replica_groups={{0,1,4,5,8,9,12,13,16,17,20,21,24,25,28,29,32,33,36,37,40,41,44,45,48,4..., dimensions={0} | all-to-all | bytes 4194304 | tf_op jit(solution)/shard_map/all_to_all | solution.py:296
  46.9 0.0 copy-done.1
  46.9 0.0 copy-start.5
  46.9 0.0 copy-start.6
  46.9 0.0 copy-start.7
  46.9 5.7 %shard_map.104 = f32[2,2,4,4,2,2,2,16,128]{8,7,6,5,4,3,2,1,0:T(8,128)S(1)} custom-call(f32[2,2,4,4,2,2,16,128]{7,6,5,4,3,2,1,0:T(8,128)S(1)} %bitcast.19, f32[2,3,136,384]{3,2,1,0:T(8,128)S(1)} %get-tuple-element.9.filters, bf16[6,256,256]{2,1,0:T(8,128)(2,1)S(1)} %copy-done.1), custom_call_target="tpu_custom_call" | custom-call | tf_op jit(solution)/shard_map/pallas_call | solution.py:282
  52.6 0.0 copy-start
  52.6 0.0 copy-start.2
  52.7 0.0 copy-start.3
  52.7 0.0 copy-start.4
  52.7 57.1 %all_to_all.11 = f32[128,64,128]{2,1,0:T(8,128)S(1)} all-to-all(f32[128,64,128]{2,1,0:T(8,128)S(1)} %bitcast.16), channel_id=1, replica_groups={{0,1,4,5,8,9,12,13,16,17,20,21,24,25,28,29,32,33,36,37,40,41,44,45,48,4..., dimensions={0} | all-to-all | bytes 8388608 | tf_op jit(solution)/shard_map/all_to_all | solution.py:296
  109.8 0.0 copy-done.5
  109.8 0.0 copy-done.6
  109.8 0.0 copy-done.7
  109.8 0.0 copy-done
  109.8 0.0 copy-done.2
  109.9 0.0 copy-done.3
  109.9 0.0 copy-done.4
  109.9 6.7 %shard_map.105 = (f32[64,2,8,512]{3,2,1,0:T(8,128)}, f32[64,2,8,512]{3,2,1,0:T(8,128)}, f32[64,2,8,512]{3,2,1,0:T(8,128)}) custom-call(f32[8192,128]{1,0:T(8,128)S(1)} %bitcast.15, bf16[6,256,256]{2,1,0:T(8,128)(2,1)S(1)} %copy-done.1, f32[64,2,8,512]{3,2,1,0:T(8,128)S(1)} %bitcast.18, f32[64,2,8,512]{3,2,1,0:T(8,128)S(1)} %bitcast.20, ...), custom_call_target="tpu_custom_call" | custom-call | tf_op jit(solution)/shard_map/pallas_call | solution.py:282
Async XLA Ops:
  5.0 41.8 %copy-start.1 = (bf16[6,256,256]{2,1,0:T(8,128)(2,1)S(1)}, bf16[6,256,256]{2,1,0:T(8,128)(2,1)}, u32[]{:S(2)}) copy-start(bf16[6,256,256]{2,1,0:T(8,128)(2,1)} %constant.68.clone.tables) | copy-start | bytes 2359300
  46.9 63.0 %copy-start.5 = (f32[64,16,512]{2,1,0:T(8,128)S(1)}, f32[64,16,512]{2,1,0:T(8,128)}, u32[]{:S(2)}) copy-start(f32[64,16,512]{2,1,0:T(8,128)} %param.12) | copy-start | bytes 6291460
  46.9 63.0 %copy-start.6 = (f32[64,16,512]{2,1,0:T(8,128)S(1)}, f32[64,16,512]{2,1,0:T(8,128)}, u32[]{:S(2)}) copy-start(f32[64,16,512]{2,1,0:T(8,128)} %param.13) | copy-start | bytes 6291460
  46.9 63.0 %copy-start.7 = (f32[64,16,512]{2,1,0:T(8,128)S(1)}, f32[64,16,512]{2,1,0:T(8,128)}, u32[]{:S(2)}) copy-start(f32[64,16,512]{2,1,0:T(8,128)} %param.14) | copy-start | bytes 6291460
  52.6 57.2 %copy-start = (f32[64,16,512]{2,1,0:T(8,128)S(1)}, f32[64,16,512]{2,1,0:T(8,128)}, u32[]{:S(2)}) copy-start(f32[64,16,512]{2,1,0:T(8,128)} %param.8) | copy-start | bytes 6291460
  52.6 57.2 %copy-start.2 = (f32[64,16,512]{2,1,0:T(8,128)S(1)}, f32[64,16,512]{2,1,0:T(8,128)}, u32[]{:S(2)}) copy-start(f32[64,16,512]{2,1,0:T(8,128)} %param.9) | copy-start | bytes 6291460
  52.7 57.2 %copy-start.3 = (f32[64,16,512]{2,1,0:T(8,128)S(1)}, f32[64,16,512]{2,1,0:T(8,128)}, u32[]{:S(2)}) copy-start(f32[64,16,512]{2,1,0:T(8,128)} %param.10) | copy-start | bytes 6291460
  52.7 57.2 %copy-start.4 = (f32[64,16,512]{2,1,0:T(8,128)S(1)}, f32[64,16,512]{2,1,0:T(8,128)}, u32[]{:S(2)}) copy-start(f32[64,16,512]{2,1,0:T(8,128)} %param.11) | copy-start | bytes 6291460

commit v3 on v2

--- a/solution.py
+++ b/solution.py
@@ -34,6 +34,7 @@
 
 
 EVEN, ODD, EVEN_BACK = 0, 2, 4
+PARTS = (1, 3)
 
 
 def cat3(high, low, axis):
@@ -123,6 +124,7 @@
         for g in range(4):
             load(h, g).wait()
         views = [field.at[h, g].reshape(512, 128) for g in range(4)]
+        blocks = [[], []]
         for group in range(2):
             near, far = [
                 side(
@@ -143,8 +145,9 @@
                 for i in range(4):
                     rows = results[p][i * 64 : i * 64 + 64]
                     block = jnp.concatenate([rows[:, :128], rows[:, 128:]], axis=0)
-                    place = p * 16 + h * 8 + group * 4 + i
-                    sent[pl.ds(place, 128, stride=32), :] = block.T
+                    blocks[p].append(block.T)
+        for p in range(2):
+            sent[:, p, h] = jnp.swapaxes(jnp.stack(blocks[p], axis=0), 0, 1)
 
 
 def plane_kernel(received, filters, tables, sent, spectrum, whole, filtered):
@@ -223,50 +226,57 @@
     targets = (pressure_next, lossy_term, image_sum)
 
     def store(h, a, part):
-        mine = pl.ds(part * 16, 16)
+        if a == 1:
+            lanes = pl.ds(part * 128, 128)
+            return pltpu.make_async_copy(
+                terms.at[h, 1, part], targets[1].at[:, h, :, lanes], out_sems.at[h, 1, part]
+            )
+        mine = pl.ds((part - 1) * 16, 32)
         return pltpu.make_async_copy(
-            outputs.at[h, a, mine], targets[a].at[mine, h], out_sems.at[h, a, part]
+            outputs.at[h, a // 2, mine], targets[a].at[mine, h], out_sems.at[h, a, part]
         )
 
+    def back_x(h, f):
+        fields = [jnp.swapaxes(received[:, f, p, h], 0, 1) for p in range(2)]
+        for group in range(2):
+            rows = [[], []]
+            for i in range(4):
+                for p in range(2):
+                    block = fields[p][group * 4 + i].T
+                    rows[p].append(side([block[:64], block[64:]]))
+            even = times_table(jnp.concatenate(rows[0], axis=0), tables, EVEN_BACK)
+            odd = times_table(jnp.concatenate(rows[1], axis=0), tables, ODD)
+            both = side([even + odd, even - odd])
+            for g in range(4):
+                view = terms.at[h, f, g].reshape(512, 128)
+                for i in range(4):
+                    view[pl.ds(group * 4 + i, 64, stride=8), :] = both[
+                        i * 64 : i * 64 + 64, g * 128 : g * 128 + 128
+                    ]
+
     for h in range(2):
-        for f in (1, 0):
-            for group in range(2):
-                rows = [[], []]
-                for i in range(4):
-                    for p in range(2):
-                        place = f * 32 + p * 16 + h * 8 + group * 4 + i
-                        block = received[pl.ds(place, 128, stride=64), :].T
-                        rows[p].append(side([block[:64], block[64:]]))
-                even = times_table(jnp.concatenate(rows[0], axis=0), tables, EVEN_BACK)
-                odd = times_table(jnp.concatenate(rows[1], axis=0), tables, ODD)
-                both = side([even + odd, even - odd])
-                for g in range(4):
-                    for i in range(4):
-                        terms[f, g, pl.ds(group * 4 + i, 64, stride=8), :] = both[
-                            i * 64 : i * 64 + 64, g * 128 : g * 128 + 128
-                        ]
-            if f:
-                for part in range(4):
-                    for y in range(part * 2, part * 2 + 2):
-                        mine = pl.ds(y * 64, 64)
-                        lossy = side([terms[1, g, mine, :] for g in range(4)])
-                        outputs[h, 1, pl.ds(y * 8, 8)] = lossy.reshape(8, 8, 512)
-                    store(h, 1, part).start()
+        back_x(h, 1)
         for part in range(4):
-            for y in range(part * 2, part * 2 + 2):
-                mine = pl.ds(y * 64, 64)
-                there = pl.ds(y * 8, 8)
-                stiff = side([terms[0, g, mine, :] for g in range(4)]).reshape(8, 8, 512)
-                lossy = outputs[h, 1, there]
+            store(h, 1, part).start()
+    for h in range(2):
+        back_x(h, 0)
+        for part in range(4):
+            for y in range(part * 16, part * 16 + 16, 8):
+                there = pl.ds(y, 8)
+                stiff, lossy = [
+                    jnp.concatenate([terms[h, f, g, there] for g in range(4)], axis=2)
+                    for f in range(2)
+                ]
                 now, prior, loss, stiffs, comp, snap, image = [s[there, h] for s in sources]
                 value = 2.0 * now - prior - stiffs * stiff + comp * (lossy - loss)
                 outputs[h, 0, there] = value
-                outputs[h, 2, there] = image + snap * value
-            store(h, 0, part).start()
-            store(h, 2, part).start()
+                outputs[h, 1, there] = image + snap * value
+            if part in PARTS:
+                for a in (0, 2):
+                    store(h, a, part).start()
     for h in range(2):
         for a in range(3):
-            for part in range(4):
+            for part in (range(4) if a == 1 else PARTS):
                 store(h, a, part).wait()
 
 
@@ -323,7 +333,7 @@
         forward_x_kernel,
         (device.reshape(1), outer(arrays[0]), outer(tables)),
         (pltpu.SMEM, pl.ANY, pl.ANY),
-        [vmem((4096, 128), f32), vmem((2, 3, 136, 384), f32)],
+        [vmem((128, 2, 2, 8, 128), f32), vmem((2, 3, 136, 384), f32)],
         [
             vmem((2, 4, 64, 8, 128), f32),
             vmem((4, 256, 256), jnp.bfloat16),
@@ -350,12 +360,12 @@
 
     outs = call(
         update_kernel,
-        (held(received.reshape(8192, 128)), held(tables), *map(held, arrays)),
+        (held(received.reshape(128, 2, 2, 2, 8, 128)), held(tables), *map(held, arrays)),
         (vmem,) * 9,
         [jax.ShapeDtypeStruct((64, 2, 8, 512), f32)] * 3,
         [
-            vmem((2, 4, 512, 128), f32),
-            vmem((2, 3, 64, 8, 512), f32),
+            vmem((2, 2, 4, 64, 8, 128), f32),
+            vmem((2, 2, 64, 8, 512), f32),
             dma((2, 3, 4)),
         ],
         16,

time: 117 us -> 115 us (0.983)
  Pallas kernels: 16.8 us -> 15 us
    pallas_call x3, Pallas kernels: 16.8 us -> 15 us  [call(): pl.pallas_call(kernel, in_specs=[pl.BlockSpec(memory_space=space) for spa...]
where the time goes in v3:
time: 115 us
  blocking collectives  99 us (86%)
  Pallas kernels  15 us (13%)
    all_to_all x2, blocking collectives, exchange(): lax.all_to_all(array, ('row', 'col'), split_axis=0, concat_axis=0, tiled=...  99 us
    pallas_call x3, Pallas kernels, call(): pl.pallas_call(kernel, in_specs=[pl.BlockSpec(memory_space=space) for spa...  15 us

profile of v3, /device:TPU:1, one launch (start us, length us, event | category | flops | bytes accessed | tf_op | source)
XLA Modules:
  0.0 114.9 jit_solution(14036993186569322900)
XLA Ops:
  0.7 3.6 %shard_map.103 = (f32[128,2,2,8,128]{4,3,2,1,0:T(8,128)S(1)}, f32[2,3,136,384]{3,2,1,0:T(8,128)S(1)}) custom-call(s32[1]{0:T(128)} %bitcast.device, f32[64,2,8,512]{3,2,1,0:T(8,128)} %bitcast.17, bf16[6,256,256]{2,1,0:T(8,128)(2,1)} %constant.68.clone.tables), custom_call_target="tpu_custom_call" | custom-call | tf_op jit(solution)/shard_map/pallas_call | solution.py:292
  4.3 0.0 copy-start.1
  4.3 41.8 %all_to_all.10 = f32[128,32,128]{2,1,0:T(8,128)S(1)} all-to-all(f32[128,32,128]{2,1,0:T(8,128)S(1)} %bitcast.26), channel_id=1, replica_groups={{0,1,4,5,8,9,12,13,16,17,20,21,24,25,28,29,32,33,36,37,40,41,44,45,48,4..., dimensions={0} | all-to-all | bytes 4194304 | tf_op jit(solution)/shard_map/all_to_all | solution.py:306
  46.2 0.0 copy-done.1
  46.2 0.0 copy-start.5
  46.2 0.0 copy-start.6
  46.2 0.0 copy-start.7
  46.2 5.7 %shard_map.104 = f32[2,2,4,4,2,2,2,16,128]{8,7,6,5,4,3,2,1,0:T(8,128)S(1)} custom-call(f32[2,2,4,4,2,2,16,128]{7,6,5,4,3,2,1,0:T(8,128)S(1)} %bitcast.19, f32[2,3,136,384]{3,2,1,0:T(8,128)S(1)} %get-tuple-element.9.filters, bf16[6,256,256]{2,1,0:T(8,128)(2,1)S(1)} %copy-done.1), custom_call_target="tpu_custom_call" | custom-call | tf_op jit(solution)/shard_map/pallas_call | solution.py:292
  51.9 0.0 copy-start
  51.9 0.0 copy-start.2
  51.9 0.0 copy-start.3
  52.0 0.0 copy-start.4
  52.0 57.1 %all_to_all.11 = f32[128,64,128]{2,1,0:T(8,128)S(1)} all-to-all(f32[128,64,128]{2,1,0:T(8,128)S(1)} %bitcast.16), channel_id=1, replica_groups={{0,1,4,5,8,9,12,13,16,17,20,21,24,25,28,29,32,33,36,37,40,41,44,45,48,4..., dimensions={0} | all-to-all | bytes 8388608 | tf_op jit(solution)/shard_map/all_to_all | solution.py:306
  109.1 0.0 copy-done.5
  109.1 0.0 copy-done.6
  109.1 0.0 copy-done.7
  109.1 0.0 copy-done
  109.1 0.0 copy-done.2
  109.1 0.0 copy-done.3
  109.2 0.0 copy-done.4
  109.2 5.6 %shard_map.105 = (f32[64,2,8,512]{3,2,1,0:T(8,128)}, f32[64,2,8,512]{3,2,1,0:T(8,128)}, f32[64,2,8,512]{3,2,1,0:T(8,128)}) custom-call(f32[128,2,2,2,8,128]{5,4,3,2,1,0:T(8,128)S(1)} %bitcast.15, bf16[6,256,256]{2,1,0:T(8,128)(2,1)S(1)} %copy-done.1, f32[64,2,8,512]{3,2,1,0:T(8,128)S(1)} %bitcast.18, f32[64,2,8,512]{3,2,1,0:T(8,128)S(1)} %bitcast.20, ...), custom_call_target="tpu_custom_call" | custom-call | tf_op jit(solution)/shard_map/pallas_call | solution.py:292
Async XLA Ops:
  4.3 41.8 %copy-start.1 = (bf16[6,256,256]{2,1,0:T(8,128)(2,1)S(1)}, bf16[6,256,256]{2,1,0:T(8,128)(2,1)}, u32[]{:S(2)}) copy-start(bf16[6,256,256]{2,1,0:T(8,128)(2,1)} %constant.68.clone.tables) | copy-start | bytes 2359300
  46.2 63.0 %copy-start.5 = (f32[64,16,512]{2,1,0:T(8,128)S(1)}, f32[64,16,512]{2,1,0:T(8,128)}, u32[]{:S(2)}) copy-start(f32[64,16,512]{2,1,0:T(8,128)} %param.12) | copy-start | bytes 6291460
  46.2 63.0 %copy-start.6 = (f32[64,16,512]{2,1,0:T(8,128)S(1)}, f32[64,16,512]{2,1,0:T(8,128)}, u32[]{:S(2)}) copy-start(f32[64,16,512]{2,1,0:T(8,128)} %param.13) | copy-start | bytes 6291460
  46.2 63.0 %copy-start.7 = (f32[64,16,512]{2,1,0:T(8,128)S(1)}, f32[64,16,512]{2,1,0:T(8,128)}, u32[]{:S(2)}) copy-start(f32[64,16,512]{2,1,0:T(8,128)} %param.14) | copy-start | bytes 6291460
  51.9 57.2 %copy-start = (f32[64,16,512]{2,1,0:T(8,128)S(1)}, f32[64,16,512]{2,1,0:T(8,128)}, u32[]{:S(2)}) copy-start(f32[64,16,512]{2,1,0:T(8,128)} %param.8) | copy-start | bytes 6291460
  51.9 57.2 %copy-start.2 = (f32[64,16,512]{2,1,0:T(8,128)S(1)}, f32[64,16,512]{2,1,0:T(8,128)}, u32[]{:S(2)}) copy-start(f32[64,16,512]{2,1,0:T(8,128)} %param.9) | copy-start | bytes 6291460
  51.9 57.2 %copy-start.3 = (f32[64,16,512]{2,1,0:T(8,128)S(1)}, f32[64,16,512]{2,1,0:T(8,128)}, u32[]{:S(2)}) copy-start(f32[64,16,512]{2,1,0:T(8,128)} %param.10) | copy-start | bytes 6291460
  52.0 57.2 %copy-start.4 = (f32[64,16,512]{2,1,0:T(8,128)S(1)}, f32[64,16,512]{2,1,0:T(8,128)}, u32[]{:S(2)}) copy-start(f32[64,16,512]{2,1,0:T(8,128)} %param.11) | copy-start | bytes 6291460

commit v4 on v3

--- a/solution.py
+++ b/solution.py
@@ -27,18 +27,19 @@
     return np.cos(angle) + np.sin(angle)
 
 
+def block_table(table):
+    high, low = split_table(table)
+    return np.block([[high, high], [low, np.zeros_like(low)]])
+
+
 def pieces(values):
     high = values.astype(jnp.bfloat16)
     low = (values - high.astype(jnp.float32)).astype(jnp.bfloat16)
     return high, low
 
 
-EVEN, ODD, EVEN_BACK = 0, 2, 4
+SPLIT, ODD, SPLIT_BACK = (0, 1), 2, (4, 5)
 PARTS = (1, 3)
-
-
-def cat3(high, low, axis):
-    return jnp.concatenate([high, low, high], axis=axis)
 
 
 def product(left, right, right_dim):
@@ -47,23 +48,32 @@
     )
 
 
-def times_table(values, tables, which, transposed=False):
+def times_odd(values, tables, transposed):
     axis = 1 if transposed else 0
-    high, low = tables[which], tables[which + 1]
-    table = jnp.concatenate([high, high, low], axis=axis)
-    return product(cat3(*pieces(values), 1), table, axis)
-
-
-def table_times(tables, which, values, transposed=False):
-    axis = 1 if transposed else 0
-    high, low = tables[which], tables[which + 1]
-    table = jnp.concatenate([high, high, low], axis=1)
-    return product(table, cat3(*pieces(values), axis), axis)
-
-
-def loop(count, step):
-    for i in range(count):
-        step(i, 0)
+    high, low = pieces(values)
+    table = jnp.concatenate([tables[ODD], tables[ODD], tables[ODD + 1]], axis=axis)
+    return product(jnp.concatenate([high, low, high], axis=1), table, axis)
+
+
+def times_block(values, table):
+    both = product(jnp.concatenate(pieces(values), axis=1), table, 1)
+    return both[:, :128] + both[:, 128:]
+
+
+def block_times(table, values):
+    both = product(table, jnp.concatenate(pieces(values), axis=0), 0)
+    return both[:128] + both[128:]
+
+
+def even_forward(values, tables):
+    near, far = values[:, :128], values[:, 128:]
+    return side([times_block(near + far, tables[SPLIT[0]]), times_block(near - far, tables[SPLIT[1]])])
+
+
+def even_back(values, tables):
+    even = times_block(values[:, :128], tables[SPLIT_BACK[0]])
+    odd = times_block(values[:, 128:], tables[SPLIT_BACK[1]])
+    return side([even + odd, even - odd])
 
 
 def swap_halves(first, second):
@@ -81,10 +91,12 @@
     normalizer = 1.0 / (512 * 256 * 512)
     lane = lax.broadcasted_iota(jnp.int32, (8, 128), 1)
     row = lax.broadcasted_iota(jnp.int32, (8, 128), 0)
-    even_y = 2 * lane
-    waves_y = [even_y, jnp.where(lane == 0, 256, even_y), even_y + 1]
-    even_x = 2 * device
-    waves_x = [even_x, jnp.where(device == 0, 256, even_x), even_x + 1]
+
+    def waves(place):
+        fourth = 4 * (place % 64)
+        return [jnp.where(place == 64, 256, fourth), fourth + 2, 2 * place + 1]
+
+    waves_y, waves_x = waves(lane), waves(device)
 
     def square(wave, length):
         return (2.0 * math.pi / length * wave.astype(jnp.float32)) ** 2
@@ -92,7 +104,7 @@
     squares_y = [square(wave, 512) for wave in waves_y]
     squares_x = [square(wave, 512) for wave in waves_x]
     for tile in range(17):
-        wave_z = row + tile * 8 if tile < 16 else jnp.where(row == 0, 128, row)
+        wave_z = 2 * (row + tile % 8 * 8) + tile // 8 if tile < 16 else jnp.where(row == 0, 128, 2 * row)
         square_z = square(wave_z, 256)
         for j in range(3):
             square_yz = squares_y[j] + square_z
@@ -138,8 +150,8 @@
                 for half in range(2)
             ]
             results = [
-                times_table(near + far, table, EVEN),
-                times_table(near - far, table, ODD, True),
+                even_forward(near + far, table),
+                times_odd(near - far, table, True),
             ]
             for p in range(2):
                 for i in range(4):
@@ -161,7 +173,14 @@
             ],
             axis=0,
         )
-        result = table_times(tables, EVEN_BACK, plane)
+        near, far = plane[:128], plane[128:]
+        result = jnp.concatenate(
+            [
+                block_times(tables[SPLIT[0]], near + far),
+                block_times(tables[SPLIT[1]], near - far),
+            ],
+            axis=0,
+        )
         for p in range(2):
             spectrum[p, r] = result[:, p * 128 : p * 128 + 128]
     for p in range(2):
@@ -173,19 +192,26 @@
         for i in range(2):
             k = p * 2 + i
             near, far = side(columns[i][:2]), side(columns[i][2:])
-            whole[k, :, :256] = times_table(near + far, tables, EVEN)
-            whole[k, :, 256:] = times_table(near - far, tables, ODD, True)
+            whole[k, :, :256] = even_forward(near + far, tables)
+            whole[k, :, 256:] = times_odd(near - far, tables, True)
     for p in range(2):
         for f in range(2):
             backs = []
             for k in (p * 2, p * 2 + 1):
                 q = min(k, 2)
                 filter_rows = jnp.concatenate(
-                    [filters[f, q, 0:128], filters[f, q, 128:136], filters[f, q, 8:128]], axis=0
+                    [
+                        filters[f, q, 0:64],
+                        filters[f, q, 128:136],
+                        filters[f, q, 8:64],
+                        filters[f, q, 64:128],
+                        filters[f, q, 64:128],
+                    ],
+                    axis=0,
                 )
                 filter_odd = side([filter_rows[:, 256:], filter_rows[:, 256:]])
-                back_even = times_table(whole[k, :, :256] * filter_rows[:, :256], tables, EVEN_BACK)
-                back_odd = times_table(whole[k, :, 256:] * filter_odd, tables, ODD)
+                back_even = even_back(whole[k, :, :256] * filter_rows[:, :256], tables)
+                back_odd = times_odd(whole[k, :, 256:] * filter_odd, tables, False)
                 backs.append(side([back_even + back_odd, back_even - back_odd]))
             for r in range(0, 8, 2):
                 part = slice(r * 64, r * 64 + 128)
@@ -195,7 +221,14 @@
     for r in range(8):
         low, y = divmod(r, 4)
         for f in range(2):
-            field = table_times(tables, EVEN, side([filtered[f, r, p] for p in range(2)]))
+            even, odd = [
+                block_times(
+                    tables[SPLIT_BACK[i]],
+                    side([filtered[f, r, p, i * 128 : i * 128 + 128] for p in range(2)]),
+                )
+                for i in range(2)
+            ]
+            field = jnp.concatenate([even + odd, even - odd], axis=0)
             for c, (high, x, core) in enumerate(chunks):
                 for p in range(2):
                     sent[high, low, y, x, core, f, p] = field[
@@ -244,8 +277,8 @@
                 for p in range(2):
                     block = fields[p][group * 4 + i].T
                     rows[p].append(side([block[:64], block[64:]]))
-            even = times_table(jnp.concatenate(rows[0], axis=0), tables, EVEN_BACK)
-            odd = times_table(jnp.concatenate(rows[1], axis=0), tables, ODD)
+            even = even_back(jnp.concatenate(rows[0], axis=0), tables)
+            odd = times_odd(jnp.concatenate(rows[1], axis=0), tables, False)
             both = side([even + odd, even - odd])
             for g in range(4):
                 view = terms.at[h, f, g].reshape(512, 128)
@@ -309,13 +342,20 @@
 
 
 def body(pressure, pressure_prior, lossy_prior, stiffness, compensation, snapshot, image_prior):
-    half = np.arange(256)
-    even_order = np.concatenate([half[:128], [128], half[:128:-1]])
-    odd_order = np.concatenate([half[:128], half[:127:-1]])
-    even_table = cas(half, even_order, 256)
-    odd_table = cas(2 * odd_order + 1, half, 512)
+    half, block = np.arange(256), np.arange(128)
+    even_order = np.concatenate([block[:64], [64], block[:64:-1]])
+    odd_order = np.concatenate([block[:64], block[:63:-1]])
+    even_table = cas(even_order, block, 128)
+    odd_table = cas(2 * odd_order + 1, block, 256)
+    last_order = np.concatenate([half[:128], half[:127:-1]])
     tables = np.stack(
-        [*split_table(even_table), *split_table(odd_table), *split_table(even_table.T)]
+        [
+            block_table(even_table),
+            block_table(odd_table),
+            *split_table(cas(2 * last_order + 1, half, 512)),
+            block_table(even_table.T),
+            block_table(odd_table.T),
+        ]
     )
     place = np.arange(128).reshape(2, 4, 4, 2, 2)
     order = [int(i) for i in place.transpose(3, 0, 1, 2, 4).reshape(-1)]

time: 115 us -> 113 us (0.983)
  Pallas kernels: 15 us -> 13.4 us
    pallas_call x3, Pallas kernels: 15 us -> 13.4 us  [call(): pl.pallas_call(kernel, in_specs=[pl.BlockSpec(memory_space=space) for spa...]
where the time goes in v4:
time: 113 us
  blocking collectives  99 us (88%)
  Pallas kernels  13.4 us (12%)
    all_to_all x2, blocking collectives, exchange(): lax.all_to_all(array, ('row', 'col'), split_axis=0, concat_axis=0, tiled=...  99 us
    pallas_call x3, Pallas kernels, call(): pl.pallas_call(kernel, in_specs=[pl.BlockSpec(memory_space=space) for spa...  13.4 us

profile of v4, /device:TPU:1, one launch (start us, length us, event | category | flops | bytes accessed | tf_op | source)
XLA Modules:
  0.0 113.2 jit_solution(7782369196431339671)
XLA Ops:
  0.7 3.5 %shard_map.103 = (f32[128,2,2,8,128]{4,3,2,1,0:T(8,128)S(1)}, f32[2,3,136,384]{3,2,1,0:T(8,128)S(1)}) custom-call(s32[1]{0:T(128)} %bitcast.device, f32[64,2,8,512]{3,2,1,0:T(8,128)} %bitcast.17, bf16[6,256,256]{2,1,0:T(8,128)(2,1)} %constant.68.clone.tables), custom_call_target="tpu_custom_call" | custom-call | tf_op jit(solution)/shard_map/pallas_call | solution.py:325
  4.2 0.0 copy-start.1
  4.2 41.8 %all_to_all.10 = f32[128,32,128]{2,1,0:T(8,128)S(1)} all-to-all(f32[128,32,128]{2,1,0:T(8,128)S(1)} %bitcast.26), channel_id=1, replica_groups={{0,1,4,5,8,9,12,13,16,17,20,21,24,25,28,29,32,33,36,37,40,41,44,45,48,4..., dimensions={0} | all-to-all | bytes 4194304 | tf_op jit(solution)/shard_map/all_to_all | solution.py:339
  46.0 0.0 copy-done.1
  46.0 0.0 copy-start.5
  46.0 0.0 copy-start.6
  46.0 0.0 copy-start.7
  46.0 4.5 %shard_map.104 = f32[2,2,4,4,2,2,2,16,128]{8,7,6,5,4,3,2,1,0:T(8,128)S(1)} custom-call(f32[2,2,4,4,2,2,16,128]{7,6,5,4,3,2,1,0:T(8,128)S(1)} %bitcast.19, f32[2,3,136,384]{3,2,1,0:T(8,128)S(1)} %get-tuple-element.9.filters, bf16[6,256,256]{2,1,0:T(8,128)(2,1)S(1)} %copy-done.1), custom_call_target="tpu_custom_call" | custom-call | tf_op jit(solution)/shard_map/pallas_call | solution.py:325
  50.5 0.0 copy-start
  50.6 0.0 copy-start.2
  50.6 0.0 copy-start.3
  50.6 0.0 copy-start.4
  50.6 57.1 %all_to_all.11 = f32[128,64,128]{2,1,0:T(8,128)S(1)} all-to-all(f32[128,64,128]{2,1,0:T(8,128)S(1)} %bitcast.16), channel_id=1, replica_groups={{0,1,4,5,8,9,12,13,16,17,20,21,24,25,28,29,32,33,36,37,40,41,44,45,48,4..., dimensions={0} | all-to-all | bytes 8388608 | tf_op jit(solution)/shard_map/all_to_all | solution.py:339
  107.7 0.0 copy-done.5
  107.7 0.0 copy-done.6
  107.7 0.0 copy-done.7
  107.7 0.0 copy-done
  107.7 0.0 copy-done.2
  107.8 0.0 copy-done.3
  107.8 0.0 copy-done.4
  107.8 5.4 %shard_map.105 = (f32[64,2,8,512]{3,2,1,0:T(8,128)}, f32[64,2,8,512]{3,2,1,0:T(8,128)}, f32[64,2,8,512]{3,2,1,0:T(8,128)}) custom-call(f32[128,2,2,2,8,128]{5,4,3,2,1,0:T(8,128)S(1)} %bitcast.15, bf16[6,256,256]{2,1,0:T(8,128)(2,1)S(1)} %copy-done.1, f32[64,2,8,512]{3,2,1,0:T(8,128)S(1)} %bitcast.18, f32[64,2,8,512]{3,2,1,0:T(8,128)S(1)} %bitcast.20, ...), custom_call_target="tpu_custom_call" | custom-call | tf_op jit(solution)/shard_map/pallas_call | solution.py:325
Async XLA Ops:
  4.2 41.8 %copy-start.1 = (bf16[6,256,256]{2,1,0:T(8,128)(2,1)S(1)}, bf16[6,256,256]{2,1,0:T(8,128)(2,1)}, u32[]{:S(2)}) copy-start(bf16[6,256,256]{2,1,0:T(8,128)(2,1)} %constant.68.clone.tables) | copy-start | bytes 2359300
  46.0 61.7 %copy-start.5 = (f32[64,16,512]{2,1,0:T(8,128)S(1)}, f32[64,16,512]{2,1,0:T(8,128)}, u32[]{:S(2)}) copy-start(f32[64,16,512]{2,1,0:T(8,128)} %param.12) | copy-start | bytes 6291460
  46.0 61.7 %copy-start.6 = (f32[64,16,512]{2,1,0:T(8,128)S(1)}, f32[64,16,512]{2,1,0:T(8,128)}, u32[]{:S(2)}) copy-start(f32[64,16,512]{2,1,0:T(8,128)} %param.13) | copy-start | bytes 6291460
  46.0 61.7 %copy-start.7 = (f32[64,16,512]{2,1,0:T(8,128)S(1)}, f32[64,16,512]{2,1,0:T(8,128)}, u32[]{:S(2)}) copy-start(f32[64,16,512]{2,1,0:T(8,128)} %param.14) | copy-start | bytes 6291460
  50.5 57.2 %copy-start = (f32[64,16,512]{2,1,0:T(8,128)S(1)}, f32[64,16,512]{2,1,0:T(8,128)}, u32[]{:S(2)}) copy-start(f32[64,16,512]{2,1,0:T(8,128)} %param.8) | copy-start | bytes 6291460
  50.6 57.2 %copy-start.2 = (f32[64,16,512]{2,1,0:T(8,128)S(1)}, f32[64,16,512]{2,1,0:T(8,128)}, u32[]{:S(2)}) copy-start(f32[64,16,512]{2,1,0:T(8,128)} %param.9) | copy-start | bytes 6291460
  50.6 57.2 %copy-start.3 = (f32[64,16,512]{2,1,0:T(8,128)S(1)}, f32[64,16,512]{2,1,0:T(8,128)}, u32[]{:S(2)}) copy-start(f32[64,16,512]{2,1,0:T(8,128)} %param.10) | copy-start | bytes 6291460
  50.6 57.2 %copy-start.4 = (f32[64,16,512]{2,1,0:T(8,128)S(1)}, f32[64,16,512]{2,1,0:T(8,128)}, u32[]{:S(2)}) copy-start(f32[64,16,512]{2,1,0:T(8,128)} %param.11) | copy-start | bytes 6291460

commit v5 on v4

--- a/solution.py
+++ b/solution.py
@@ -29,7 +29,7 @@
 
 def block_table(table):
     high, low = split_table(table)
-    return np.block([[high, high], [low, np.zeros_like(low)]])
+    return np.block([[high, high], [low, low]])
 
 
 def pieces(values):
@@ -48,11 +48,14 @@
     )
 
 
-def times_odd(values, tables, transposed):
-    axis = 1 if transposed else 0
-    high, low = pieces(values)
-    table = jnp.concatenate([tables[ODD], tables[ODD], tables[ODD + 1]], axis=axis)
-    return product(jnp.concatenate([high, low, high], axis=1), table, axis)
+def times_odd(values, tables, forward):
+    axis = 1 if forward else 0
+    left, table = list(pieces(values)), [tables[ODD], tables[ODD], tables[ODD + 1]]
+    left.append(left[0])
+    if forward:
+        left.append(left[1])
+        table.append(tables[ODD + 1])
+    return product(jnp.concatenate(left, axis=1), jnp.concatenate(table, axis=axis), axis)
 
 
 def times_block(values, table):

time: 113 us -> 114 us (level)
  no operation moved by 1% of the time
where the time goes in v5:
time: 114 us; the launch traced here: 113 us
  blocking collectives  99 us (87%)
  Pallas kernels  13.6 us (12%)
    all_to_all x2, blocking collectives, exchange(): lax.all_to_all(array, ('row', 'col'), split_axis=0, concat_axis=0, tiled=...  99 us
    pallas_call x3, Pallas kernels, call(): pl.pallas_call(kernel, in_specs=[pl.BlockSpec(memory_space=space) for spa...  13.6 us

profile of v5, /device:TPU:1, one launch (start us, length us, event | category | flops | bytes accessed | tf_op | source)
XLA Modules:
  0.0 113.4 jit_solution(13433148899861092820)
XLA Ops:
  0.7 3.6 %shard_map.103 = (f32[128,2,2,8,128]{4,3,2,1,0:T(8,128)S(1)}, f32[2,3,136,384]{3,2,1,0:T(8,128)S(1)}) custom-call(s32[1]{0:T(128)} %bitcast.device, f32[64,2,8,512]{3,2,1,0:T(8,128)} %bitcast.17, bf16[6,256,256]{2,1,0:T(8,128)(2,1)} %constant.68.clone.tables), custom_call_target="tpu_custom_call" | custom-call | tf_op jit(solution)/shard_map/pallas_call | solution.py:328
  4.3 0.0 copy-start.1
  4.3 41.8 %all_to_all.10 = f32[128,32,128]{2,1,0:T(8,128)S(1)} all-to-all(f32[128,32,128]{2,1,0:T(8,128)S(1)} %bitcast.26), channel_id=1, replica_groups={{0,1,4,5,8,9,12,13,16,17,20,21,24,25,28,29,32,33,36,37,40,41,44,45,48,4..., dimensions={0} | all-to-all | bytes 4194304 | tf_op jit(solution)/shard_map/all_to_all | solution.py:342
  46.1 0.0 copy-done.1
  46.2 0.0 copy-start.5
  46.2 0.0 copy-start.6
  46.2 0.0 copy-start.7
  46.2 4.6 %shard_map.104 = f32[2,2,4,4,2,2,2,16,128]{8,7,6,5,4,3,2,1,0:T(8,128)S(1)} custom-call(f32[2,2,4,4,2,2,16,128]{7,6,5,4,3,2,1,0:T(8,128)S(1)} %bitcast.19, f32[2,3,136,384]{3,2,1,0:T(8,128)S(1)} %get-tuple-element.9.filters, bf16[6,256,256]{2,1,0:T(8,128)(2,1)S(1)} %copy-done.1), custom_call_target="tpu_custom_call" | custom-call | tf_op jit(solution)/shard_map/pallas_call | solution.py:328
  50.8 0.0 copy-start
  50.8 0.0 copy-start.2
  50.8 0.0 copy-start.3
  50.8 0.0 copy-start.4
  50.8 57.1 %all_to_all.11 = f32[128,64,128]{2,1,0:T(8,128)S(1)} all-to-all(f32[128,64,128]{2,1,0:T(8,128)S(1)} %bitcast.16), channel_id=1, replica_groups={{0,1,4,5,8,9,12,13,16,17,20,21,24,25,28,29,32,33,36,37,40,41,44,45,48,4..., dimensions={0} | all-to-all | bytes 8388608 | tf_op jit(solution)/shard_map/all_to_all | solution.py:342
  108.0 0.0 copy-done.5
  108.0 0.0 copy-done.6
  108.0 0.0 copy-done.7
  108.0 0.0 copy-done
  108.0 0.0 copy-done.2
  108.0 0.0 copy-done.3
  108.0 0.0 copy-done.4
  108.0 5.4 %shard_map.105 = (f32[64,2,8,512]{3,2,1,0:T(8,128)}, f32[64,2,8,512]{3,2,1,0:T(8,128)}, f32[64,2,8,512]{3,2,1,0:T(8,128)}) custom-call(f32[128,2,2,2,8,128]{5,4,3,2,1,0:T(8,128)S(1)} %bitcast.15, bf16[6,256,256]{2,1,0:T(8,128)(2,1)S(1)} %copy-done.1, f32[64,2,8,512]{3,2,1,0:T(8,128)S(1)} %bitcast.18, f32[64,2,8,512]{3,2,1,0:T(8,128)S(1)} %bitcast.20, ...), custom_call_target="tpu_custom_call" | custom-call | tf_op jit(solution)/shard_map/pallas_call | solution.py:328
Async XLA Ops:
  4.3 41.8 %copy-start.1 = (bf16[6,256,256]{2,1,0:T(8,128)(2,1)S(1)}, bf16[6,256,256]{2,1,0:T(8,128)(2,1)}, u32[]{:S(2)}) copy-start(bf16[6,256,256]{2,1,0:T(8,128)(2,1)} %constant.68.clone.tables) | copy-start | bytes 2359300
  46.2 61.8 %copy-start.5 = (f32[64,16,512]{2,1,0:T(8,128)S(1)}, f32[64,16,512]{2,1,0:T(8,128)}, u32[]{:S(2)}) copy-start(f32[64,16,512]{2,1,0:T(8,128)} %param.12) | copy-start | bytes 6291460
  46.2 61.8 %copy-start.6 = (f32[64,16,512]{2,1,0:T(8,128)S(1)}, f32[64,16,512]{2,1,0:T(8,128)}, u32[]{:S(2)}) copy-start(f32[64,16,512]{2,1,0:T(8,128)} %param.13) | copy-start | bytes 6291460
  46.2 61.8 %copy-start.7 = (f32[64,16,512]{2,1,0:T(8,128)S(1)}, f32[64,16,512]{2,1,0:T(8,128)}, u32[]{:S(2)}) copy-start(f32[64,16,512]{2,1,0:T(8,128)} %param.14) | copy-start | bytes 6291460
  50.8 57.2 %copy-start = (f32[64,16,512]{2,1,0:T(8,128)S(1)}, f32[64,16,512]{2,1,0:T(8,128)}, u32[]{:S(2)}) copy-start(f32[64,16,512]{2,1,0:T(8,128)} %param.8) | copy-start | bytes 6291460
  50.8 57.2 %copy-start.2 = (f32[64,16,512]{2,1,0:T(8,128)S(1)}, f32[64,16,512]{2,1,0:T(8,128)}, u32[]{:S(2)}) copy-start(f32[64,16,512]{2,1,0:T(8,128)} %param.9) | copy-start | bytes 6291460
  50.8 57.2 %copy-start.3 = (f32[64,16,512]{2,1,0:T(8,128)S(1)}, f32[64,16,512]{2,1,0:T(8,128)}, u32[]{:S(2)}) copy-start(f32[64,16,512]{2,1,0:T(8,128)} %param.10) | copy-start | bytes 6291460
  50.8 57.2 %copy-start.4 = (f32[64,16,512]{2,1,0:T(8,128)S(1)}, f32[64,16,512]{2,1,0:T(8,128)}, u32[]{:S(2)}) copy-start(f32[64,16,512]{2,1,0:T(8,128)} %param.11) | copy-start | bytes 6291460

commit v6 on v4

--- a/solution.py
+++ b/solution.py
@@ -29,7 +29,13 @@
 
 def block_table(table):
     high, low = split_table(table)
-    return np.block([[high, high], [low, np.zeros_like(low)]])
+    return np.block([[high, high], [low, low]])
+
+
+def rest_table(table):
+    high, low = split_table(table)
+    rest = (table - high.astype(np.float64) - low.astype(np.float64)).astype(ml_dtypes.bfloat16)
+    return np.block([[high, rest], [np.zeros_like(high), np.zeros_like(high)]])
 
 
 def pieces(values):
@@ -38,7 +44,7 @@
     return high, low
 
 
-SPLIT, ODD, SPLIT_BACK = (0, 1), 2, (4, 5)
+SPLIT, ODD, SPLIT_REST, SPLIT_BACK = (0, 1), 2, (5, 6), (7, 8)
 PARTS = (1, 3)
 
 
@@ -48,31 +54,62 @@
     )
 
 
-def times_odd(values, tables, transposed):
-    axis = 1 if transposed else 0
+def three_pieces(values):
     high, low = pieces(values)
-    table = jnp.concatenate([tables[ODD], tables[ODD], tables[ODD + 1]], axis=axis)
-    return product(jnp.concatenate([high, low, high], axis=1), table, axis)
-
-
-def times_block(values, table):
-    both = product(jnp.concatenate(pieces(values), axis=1), table, 1)
+    rest = values - high.astype(jnp.float32) - low.astype(jnp.float32)
+    return high, low, rest.astype(jnp.bfloat16)
+
+
+def odd_forward(values, tables):
+    high, low, rest = three_pieces(values)
+    first, second, third = [tables[ODD + i] for i in range(3)]
+    left = side([high, low, high, low, rest, high])
+    return product(left, side([first, first, second, second, first, third]), 1)
+
+
+def odd_back(values, tables):
+    high, low = pieces(values)
+    table = jnp.concatenate([tables[ODD], tables[ODD], tables[ODD + 1]], axis=0)
+    return product(side([high, low, high]), table, 0)
+
+
+def forward_table(tables, i):
+    return side([tables[SPLIT[i]], tables[SPLIT_REST[i]]])
+
+
+def times_block(values, table, forward):
+    if forward:
+        high, low, rest = three_pieces(values)
+        left = side([high, low, rest, high])
+    else:
+        left = side(pieces(values))
+    both = product(left, table, 1)
     return both[:, :128] + both[:, 128:]
 
 
-def block_times(table, values):
-    both = product(table, jnp.concatenate(pieces(values), axis=0), 0)
-    return both[:128] + both[128:]
+def block_times(table, values, rest_table=None):
+    if rest_table is None:
+        both = product(table, jnp.concatenate(pieces(values), axis=0), 0)
+        return both[:128] + both[128:]
+    high, low, rest = three_pieces(values)
+    both = product(table, jnp.concatenate([high, low], axis=0), 0)
+    third = product(rest_table[:128], jnp.concatenate([rest, high], axis=0), 0)
+    return both[:128] + (both[128:] + third)
 
 
 def even_forward(values, tables):
     near, far = values[:, :128], values[:, 128:]
-    return side([times_block(near + far, tables[SPLIT[0]]), times_block(near - far, tables[SPLIT[1]])])
+    return side(
+        [
+            times_block(near + far, forward_table(tables, 0), True),
+            times_block(near - far, forward_table(tables, 1), True),
+        ]
+    )
 
 
 def even_back(values, tables):
-    even = times_block(values[:, :128], tables[SPLIT_BACK[0]])
-    odd = times_block(values[:, 128:], tables[SPLIT_BACK[1]])
+    even = times_block(values[:, :128], tables[SPLIT_BACK[0]], False)
+    odd = times_block(values[:, 128:], tables[SPLIT_BACK[1]], False)
     return side([even + odd, even - odd])
 
 
@@ -124,7 +161,7 @@
             pressure.at[:, h, :, pl.ds(g * 128, 128)], field.at[h, g], in_sems.at[h, g]
         )
 
-    load_table = pltpu.make_async_copy(tables.at[pl.ds(0, 4)], table, table_sem)
+    load_table = pltpu.make_async_copy(tables.at[pl.ds(0, 7)], table, table_sem)
     for g in range(4):
         load(0, g).start()
     load_table.start()
@@ -151,7 +188,7 @@
             ]
             results = [
                 even_forward(near + far, table),
-                times_odd(near - far, table, True),
+                odd_forward(near - far, table),
             ]
             for p in range(2):
                 for i in range(4):
@@ -176,8 +213,8 @@
         near, far = plane[:128], plane[128:]
         result = jnp.concatenate(
             [
-                block_times(tables[SPLIT[0]], near + far),
-                block_times(tables[SPLIT[1]], near - far),
+                block_times(tables[SPLIT[0]], near + far, tables[SPLIT_REST[0]]),
+                block_times(tables[SPLIT[1]], near - far, tables[SPLIT_REST[1]]),
             ],
             axis=0,
         )
@@ -193,7 +230,7 @@
             k = p * 2 + i
             near, far = side(columns[i][:2]), side(columns[i][2:])
             whole[k, :, :256] = even_forward(near + far, tables)
-            whole[k, :, 256:] = times_odd(near - far, tables, True)
+            whole[k, :, 256:] = odd_forward(near - far, tables)
     for p in range(2):
         for f in range(2):
             backs = []
@@ -211,7 +248,7 @@
                 )
                 filter_odd = side([filter_rows[:, 256:], filter_rows[:, 256:]])
                 back_even = even_back(whole[k, :, :256] * filter_rows[:, :256], tables)
-                back_odd = times_odd(whole[k, :, 256:] * filter_odd, tables, False)
+                back_odd = odd_back(whole[k, :, 256:] * filter_odd, tables)
                 backs.append(side([back_even + back_odd, back_even - back_odd]))
             for r in range(0, 8, 2):
                 part = slice(r * 64, r * 64 + 128)
@@ -278,7 +315,7 @@
                     block = fields[p][group * 4 + i].T
                     rows[p].append(side([block[:64], block[64:]]))
             even = even_back(jnp.concatenate(rows[0], axis=0), tables)
-            odd = times_odd(jnp.concatenate(rows[1], axis=0), tables, False)
+            odd = odd_back(jnp.concatenate(rows[1], axis=0), tables)
             both = side([even + odd, even - odd])
             for g in range(4):
                 view = terms.at[h, f, g].reshape(512, 128)
@@ -348,11 +385,15 @@
     even_table = cas(even_order, block, 128)
     odd_table = cas(2 * odd_order + 1, block, 256)
     last_order = np.concatenate([half[:128], half[:127:-1]])
+    last_table = cas(2 * last_order + 1, half, 512)
     tables = np.stack(
         [
             block_table(even_table),
             block_table(odd_table),
-            *split_table(cas(2 * last_order + 1, half, 512)),
+            *split_table(last_table),
+            rest_table(last_table)[:256, 256:],
+            rest_table(even_table),
+            rest_table(odd_table),
             block_table(even_table.T),
             block_table(odd_table.T),
         ]
@@ -376,7 +417,7 @@
         [vmem((128, 2, 2, 8, 128), f32), vmem((2, 3, 136, 384), f32)],
         [
             vmem((2, 4, 64, 8, 128), f32),
-            vmem((4, 256, 256), jnp.bfloat16),
+            vmem((7, 256, 256), jnp.bfloat16),
             dma((2, 4)),
             dma,
         ],

time: 113 us -> 115 us (1.018)
  Pallas kernels: 13.4 us -> 15.2 us
    pallas_call x3, Pallas kernels: 13.4 us -> 15.2 us  [call(): pl.pallas_call(kernel, in_specs=[pl.BlockSpec(memory_space=space) for spa...]
where the time goes in v6:
time: 115 us
  blocking collectives  99 us (86%)
  Pallas kernels  15.2 us (13%)
    all_to_all x2, blocking collectives, exchange(): lax.all_to_all(array, ('row', 'col'), split_axis=0, concat_axis=0, tiled=...  99 us
    pallas_call x3, Pallas kernels, call(): pl.pallas_call(kernel, in_specs=[pl.BlockSpec(memory_space=space) for spa...  15.2 us

profile of v6, /device:TPU:1, one launch (start us, length us, event | category | flops | bytes accessed | tf_op | source)
XLA Modules:
  0.0 115.2 jit_solution(17827097446553936321)
XLA Ops:
  0.7 4.3 %shard_map.103 = (f32[128,2,2,8,128]{4,3,2,1,0:T(8,128)S(1)}, f32[2,3,136,384]{3,2,1,0:T(8,128)S(1)}) custom-call(s32[1]{0:T(128)} %bitcast.device, f32[64,2,8,512]{3,2,1,0:T(8,128)} %bitcast.17, bf16[9,256,256]{2,1,0:T(8,128)(2,1)} %constant.68.clone.tables), custom_call_target="tpu_custom_call" | custom-call | tf_op jit(solution)/shard_map/pallas_call | solution.py:362
  5.0 0.0 copy-start
  5.0 41.8 %all_to_all.10 = f32[128,32,128]{2,1,0:T(8,128)S(1)} all-to-all(f32[128,32,128]{2,1,0:T(8,128)S(1)} %bitcast.26), channel_id=1, replica_groups={{0,1,4,5,8,9,12,13,16,17,20,21,24,25,28,29,32,33,36,37,40,41,44,45,48,4..., dimensions={0} | all-to-all | bytes 4194304 | tf_op jit(solution)/shard_map/all_to_all | solution.py:376
  46.8 0.0 copy-done
  46.8 0.0 copy-start.5
  46.8 0.0 copy-start.6
  46.8 0.0 copy-start.7
  46.8 5.5 %shard_map.104 = f32[2,2,4,4,2,2,2,16,128]{8,7,6,5,4,3,2,1,0:T(8,128)S(1)} custom-call(f32[2,2,4,4,2,2,16,128]{7,6,5,4,3,2,1,0:T(8,128)S(1)} %bitcast.19, f32[2,3,136,384]{3,2,1,0:T(8,128)S(1)} %get-tuple-element.9.filters, bf16[9,256,256]{2,1,0:T(8,128)(2,1)S(1)} %copy-done), custom_call_target="tpu_custom_call" | custom-call | tf_op jit(solution)/shard_map/pallas_call | solution.py:362
  52.3 0.0 copy-start.1
  52.4 0.0 copy-start.2
  52.4 0.0 copy-start.3
  52.4 0.0 copy-start.4
  52.4 57.1 %all_to_all.11 = f32[128,64,128]{2,1,0:T(8,128)S(1)} all-to-all(f32[128,64,128]{2,1,0:T(8,128)S(1)} %bitcast.16), channel_id=1, replica_groups={{0,1,4,5,8,9,12,13,16,17,20,21,24,25,28,29,32,33,36,37,40,41,44,45,48,4..., dimensions={0} | all-to-all | bytes 8388608 | tf_op jit(solution)/shard_map/all_to_all | solution.py:376
  109.5 0.0 copy-done.5
  109.5 0.0 copy-done.6
  109.5 0.0 copy-done.7
  109.5 0.0 copy-done.1
  109.6 0.0 copy-done.2
  109.6 0.0 copy-done.3
  109.6 0.0 copy-done.4
  109.6 5.4 %shard_map.105 = (f32[64,2,8,512]{3,2,1,0:T(8,128)}, f32[64,2,8,512]{3,2,1,0:T(8,128)}, f32[64,2,8,512]{3,2,1,0:T(8,128)}) custom-call(f32[128,2,2,2,8,128]{5,4,3,2,1,0:T(8,128)S(1)} %bitcast.15, bf16[9,256,256]{2,1,0:T(8,128)(2,1)S(1)} %copy-done, f32[64,2,8,512]{3,2,1,0:T(8,128)S(1)} %bitcast.18, f32[64,2,8,512]{3,2,1,0:T(8,128)S(1)} %bitcast.20, ...), custom_call_target="tpu_custom_call" | custom-call | tf_op jit(solution)/shard_map/pallas_call | solution.py:362
Async XLA Ops:
  5.0 41.8 %copy-start = (bf16[9,256,256]{2,1,0:T(8,128)(2,1)S(1)}, bf16[9,256,256]{2,1,0:T(8,128)(2,1)}, u32[]{:S(2)}) copy-start(bf16[9,256,256]{2,1,0:T(8,128)(2,1)} %constant.68.clone.tables) | copy-start | bytes 3538948
  46.8 62.7 %copy-start.5 = (f32[64,16,512]{2,1,0:T(8,128)S(1)}, f32[64,16,512]{2,1,0:T(8,128)}, u32[]{:S(2)}) copy-start(f32[64,16,512]{2,1,0:T(8,128)} %param.12) | copy-start | bytes 6291460
  46.8 62.7 %copy-start.6 = (f32[64,16,512]{2,1,0:T(8,128)S(1)}, f32[64,16,512]{2,1,0:T(8,128)}, u32[]{:S(2)}) copy-start(f32[64,16,512]{2,1,0:T(8,128)} %param.13) | copy-start | bytes 6291460
  46.8 62.7 %copy-start.7 = (f32[64,16,512]{2,1,0:T(8,128)S(1)}, f32[64,16,512]{2,1,0:T(8,128)}, u32[]{:S(2)}) copy-start(f32[64,16,512]{2,1,0:T(8,128)} %param.14) | copy-start | bytes 6291460
  52.3 57.2 %copy-start.1 = (f32[64,16,512]{2,1,0:T(8,128)S(1)}, f32[64,16,512]{2,1,0:T(8,128)}, u32[]{:S(2)}) copy-start(f32[64,16,512]{2,1,0:T(8,128)} %param.8) | copy-start | bytes 6291460
  52.4 57.2 %copy-start.2 = (f32[64,16,512]{2,1,0:T(8,128)S(1)}, f32[64,16,512]{2,1,0:T(8,128)}, u32[]{:S(2)}) copy-start(f32[64,16,512]{2,1,0:T(8,128)} %param.9) | copy-start | bytes 6291460
  52.4 57.2 %copy-start.3 = (f32[64,16,512]{2,1,0:T(8,128)S(1)}, f32[64,16,512]{2,1,0:T(8,128)}, u32[]{:S(2)}) copy-start(f32[64,16,512]{2,1,0:T(8,128)} %param.10) | copy-start | bytes 6291460
  52.4 57.2 %copy-start.4 = (f32[64,16,512]{2,1,0:T(8,128)S(1)}, f32[64,16,512]{2,1,0:T(8,128)}, u32[]{:S(2)}) copy-start(f32[64,16,512]{2,1,0:T(8,128)} %param.11) | copy-start | bytes 6291460

commit v7 on v6

--- a/solution.py
+++ b/solution.py
@@ -326,6 +326,7 @@
 
     for h in range(2):
         back_x(h, 1)
+    for h in range(2):
         for part in range(4):
             store(h, 1, part).start()
     for h in range(2):

time: 115 us -> 115 us (level)
  no operation moved by 1% of the time
where the time goes in v7:
time: 115 us
  blocking collectives  99 us (86%)
  Pallas kernels  15.2 us (13%)
    all_to_all x2, blocking collectives, exchange(): lax.all_to_all(array, ('row', 'col'), split_axis=0, concat_axis=0, tiled=...  99 us
    pallas_call x3, Pallas kernels, call(): pl.pallas_call(kernel, in_specs=[pl.BlockSpec(memory_space=space) for spa...  15.2 us

profile of v7, /device:TPU:1, one launch (start us, length us, event | category | flops | bytes accessed | tf_op | source)
XLA Modules:
  0.0 115.2 jit_solution(10684301971768296929)
XLA Ops:
  0.7 4.3 %shard_map.103 = (f32[128,2,2,8,128]{4,3,2,1,0:T(8,128)S(1)}, f32[2,3,136,384]{3,2,1,0:T(8,128)S(1)}) custom-call(s32[1]{0:T(128)} %bitcast.device, f32[64,2,8,512]{3,2,1,0:T(8,128)} %bitcast.17, bf16[9,256,256]{2,1,0:T(8,128)(2,1)} %constant.68.clone.tables), custom_call_target="tpu_custom_call" | custom-call | tf_op jit(solution)/shard_map/pallas_call | solution.py:363
  5.0 0.0 copy-start
  5.0 41.8 %all_to_all.10 = f32[128,32,128]{2,1,0:T(8,128)S(1)} all-to-all(f32[128,32,128]{2,1,0:T(8,128)S(1)} %bitcast.26), channel_id=1, replica_groups={{0,1,4,5,8,9,12,13,16,17,20,21,24,25,28,29,32,33,36,37,40,41,44,45,48,4..., dimensions={0} | all-to-all | bytes 4194304 | tf_op jit(solution)/shard_map/all_to_all | solution.py:377
  46.8 0.0 copy-done
  46.8 0.0 copy-start.5
  46.8 0.0 copy-start.6
  46.8 0.0 copy-start.7
  46.8 5.5 %shard_map.104 = f32[2,2,4,4,2,2,2,16,128]{8,7,6,5,4,3,2,1,0:T(8,128)S(1)} custom-call(f32[2,2,4,4,2,2,16,128]{7,6,5,4,3,2,1,0:T(8,128)S(1)} %bitcast.19, f32[2,3,136,384]{3,2,1,0:T(8,128)S(1)} %get-tuple-element.9.filters, bf16[9,256,256]{2,1,0:T(8,128)(2,1)S(1)} %copy-done), custom_call_target="tpu_custom_call" | custom-call | tf_op jit(solution)/shard_map/pallas_call | solution.py:363
  52.3 0.0 copy-start.1
  52.4 0.0 copy-start.2
  52.4 0.0 copy-start.3
  52.4 0.0 copy-start.4
  52.4 57.1 %all_to_all.11 = f32[128,64,128]{2,1,0:T(8,128)S(1)} all-to-all(f32[128,64,128]{2,1,0:T(8,128)S(1)} %bitcast.16), channel_id=1, replica_groups={{0,1,4,5,8,9,12,13,16,17,20,21,24,25,28,29,32,33,36,37,40,41,44,45,48,4..., dimensions={0} | all-to-all | bytes 8388608 | tf_op jit(solution)/shard_map/all_to_all | solution.py:377
  109.5 0.0 copy-done.5
  109.5 0.0 copy-done.6
  109.5 0.0 copy-done.7
  109.5 0.0 copy-done.1
  109.6 0.0 copy-done.2
  109.6 0.0 copy-done.3
  109.6 0.0 copy-done.4
  109.6 5.4 %shard_map.105 = (f32[64,2,8,512]{3,2,1,0:T(8,128)}, f32[64,2,8,512]{3,2,1,0:T(8,128)}, f32[64,2,8,512]{3,2,1,0:T(8,128)}) custom-call(f32[128,2,2,2,8,128]{5,4,3,2,1,0:T(8,128)S(1)} %bitcast.15, bf16[9,256,256]{2,1,0:T(8,128)(2,1)S(1)} %copy-done, f32[64,2,8,512]{3,2,1,0:T(8,128)S(1)} %bitcast.18, f32[64,2,8,512]{3,2,1,0:T(8,128)S(1)} %bitcast.20, ...), custom_call_target="tpu_custom_call" | custom-call | tf_op jit(solution)/shard_map/pallas_call | solution.py:363
Async XLA Ops:
  5.0 41.8 %copy-start = (bf16[9,256,256]{2,1,0:T(8,128)(2,1)S(1)}, bf16[9,256,256]{2,1,0:T(8,128)(2,1)}, u32[]{:S(2)}) copy-start(bf16[9,256,256]{2,1,0:T(8,128)(2,1)} %constant.68.clone.tables) | copy-start | bytes 3538948
  46.8 62.7 %copy-start.5 = (f32[64,16,512]{2,1,0:T(8,128)S(1)}, f32[64,16,512]{2,1,0:T(8,128)}, u32[]{:S(2)}) copy-start(f32[64,16,512]{2,1,0:T(8,128)} %param.12) | copy-start | bytes 6291460
  46.8 62.7 %copy-start.6 = (f32[64,16,512]{2,1,0:T(8,128)S(1)}, f32[64,16,512]{2,1,0:T(8,128)}, u32[]{:S(2)}) copy-start(f32[64,16,512]{2,1,0:T(8,128)} %param.13) | copy-start | bytes 6291460
  46.8 62.7 %copy-start.7 = (f32[64,16,512]{2,1,0:T(8,128)S(1)}, f32[64,16,512]{2,1,0:T(8,128)}, u32[]{:S(2)}) copy-start(f32[64,16,512]{2,1,0:T(8,128)} %param.14) | copy-start | bytes 6291460
  52.3 57.2 %copy-start.1 = (f32[64,16,512]{2,1,0:T(8,128)S(1)}, f32[64,16,512]{2,1,0:T(8,128)}, u32[]{:S(2)}) copy-start(f32[64,16,512]{2,1,0:T(8,128)} %param.8) | copy-start | bytes 6291460
  52.4 57.2 %copy-start.2 = (f32[64,16,512]{2,1,0:T(8,128)S(1)}, f32[64,16,512]{2,1,0:T(8,128)}, u32[]{:S(2)}) copy-start(f32[64,16,512]{2,1,0:T(8,128)} %param.9) | copy-start | bytes 6291460
  52.4 57.2 %copy-start.3 = (f32[64,16,512]{2,1,0:T(8,128)S(1)}, f32[64,16,512]{2,1,0:T(8,128)}, u32[]{:S(2)}) copy-start(f32[64,16,512]{2,1,0:T(8,128)} %param.10) | copy-start | bytes 6291460
  52.4 57.2 %copy-start.4 = (f32[64,16,512]{2,1,0:T(8,128)S(1)}, f32[64,16,512]{2,1,0:T(8,128)}, u32[]{:S(2)}) copy-start(f32[64,16,512]{2,1,0:T(8,128)} %param.11) | copy-start | bytes 6291460
